TPU v7x, 32 devices: a whole 2x2x4 slice. The times are simulated.
32 devices in a mesh: dp: 4 (over y, x), gz: 8 (over z, core).
Axes of the slice: x: 2, y: 2, z: 4, core: 2. Of those that a mesh axis runs over, the one named last changes fastest.
Arguments:
- fields: bfloat16 [4, 64, 16, 128, 128], P('dp', 'gz'), may hold values from -6 to 6
- cotangent: bfloat16 [4, 64, 16, 128, 128], P('dp', 'gz'), may hold values from -6 to 6
- spectral_weight: bfloat16 [2, 16, 16, 32768], P(None, None, None, 'gz'), may hold values from -1.5 to 1.5
- pointwise_weight: bfloat16 [16, 16], replicated, may hold values from -1.5 to 1.5
Outputs:
- layer_output: bfloat16 [4, 64, 16, 128, 128], P('dp', 'gz')
- input_grad: bfloat16 [4, 64, 16, 128, 128], P('dp', 'gz')
- pointwise_grad: float32 [16, 16], replicated
- spectral_grad: float32 [2, 16, 16, 32768], P(None, None, None, 'gz')
All inputs are finite; a program needn't handle non-finite values.
Results may differ from a plain program's by a relative error of at most 0.001.
Values sent between devices are 32-bit elements; how exact they have to be, the bound alone decides.
No kernel may reach another device: no remote copies, remote signals or barrier semaphores. Data moves between devices by JAX's collectives and lax.ppermute only.
A program may use at most 128 MiB of HBM per device.

v0:
```python
import math

import jax
import jax.numpy as jnp
from jax import lax
from jax.sharding import PartitionSpec as P

M = 32


HIGHEST = lax.Precision.HIGHEST


def angle_table(length, modes, first, count):
    positions = first + jnp.arange(count, dtype=jnp.int32)
    frequency = jnp.arange(modes, dtype=jnp.int32)
    phase = positions[:, None] * frequency[None, :] % length
    angles = phase.astype(jnp.float32) * (2.0 * math.pi / length)
    return (jnp.cos(angles), jnp.sin(angles))


def plane_forward(field, cos_x, sin_x, cos_y, sin_y):
    modes = cos_x.shape[1]
    section = jnp.einsum(
        "szcxy,yb->szcxb", field, jnp.concatenate([cos_y, -sin_y], axis=1), precision=HIGHEST
    )
    block = jnp.einsum(
        "szcxb,xa->szcab", section, jnp.concatenate([cos_x, -sin_x], axis=1), precision=HIGHEST
    )
    real_part = block[..., :modes, :modes] - block[..., modes:, modes:]
    imag_part = block[..., :modes, modes:] + block[..., modes:, :modes]
    shape = real_part.shape[:3] + (modes * modes,)
    return jnp.stack([real_part.reshape(shape), imag_part.reshape(shape)])


def depth_forward(planes, cos_z, sin_z):

    def contract(values, table):
        return jnp.einsum("szcp,zk->scpk", values, table, precision=HIGHEST)

    real_out = contract(planes[0], cos_z) + contract(planes[1], sin_z)
    imag_out = contract(planes[1], cos_z) - contract(planes[0], sin_z)
    shape = real_out.shape[:2] + (real_out.shape[2] * real_out.shape[3],)
    return jnp.stack([real_out.reshape(shape), imag_out.reshape(shape)])


def depth_inverse(spectrum, cos_z, sin_z):
    modes = cos_z.shape[1]
    shape = spectrum.shape[1:3] + (spectrum.shape[3] // modes, modes)
    real_in = spectrum[0].reshape(shape)
    imag_in = spectrum[1].reshape(shape)

    def expand(values, table):
        return jnp.einsum("scpk,zk->szcp", values, table, precision=HIGHEST)

    real_out = expand(real_in, cos_z) - expand(imag_in, sin_z)
    imag_out = expand(real_in, sin_z) + expand(imag_in, cos_z)
    return jnp.stack([real_out, imag_out])


def plane_inverse(planes, cos_x, sin_x, cos_y, sin_y):
    modes = cos_x.shape[1]
    shape = planes.shape[1:4] + (modes, modes)
    real_in = planes[0].reshape(shape)
    imag_in = planes[1].reshape(shape)

    def spread(values, table):
        return jnp.einsum("szcab,xa->szcxb", values, table, precision=HIGHEST)

    real_mid = spread(real_in, cos_x) - spread(imag_in, sin_x)
    imag_mid = spread(real_in, sin_x) + spread(imag_in, cos_x)
    joined = jnp.concatenate([real_mid, imag_mid], axis=-1)
    return jnp.einsum(
        "szcxb,yb->szcxy", joined, jnp.concatenate([cos_y, -sin_y], axis=1), precision=HIGHEST
    )


def mix_modes(spectrum, weight):

    def term(values, table):
        return jnp.einsum("scm,com->som", values, table, precision=HIGHEST)

    real_out = term(spectrum[0], weight[0]) - term(spectrum[1], weight[1])
    imag_out = term(spectrum[0], weight[1]) + term(spectrum[1], weight[0])
    return jnp.stack([real_out, imag_out])


def mix_adjoint(grad_spec, weight):

    def term(values, table):
        return jnp.einsum("som,com->scm", values, table, precision=HIGHEST)

    real_out = term(grad_spec[0], weight[0]) + term(grad_spec[1], weight[1])
    imag_out = term(grad_spec[1], weight[0]) - term(grad_spec[0], weight[1])
    return jnp.stack([real_out, imag_out])


def mix_weight_grad(spectrum, grad_spec):

    def term(values, other):
        return jnp.einsum("scm,som->com", values, other, precision=HIGHEST)

    real_out = term(spectrum[0], grad_spec[0]) + term(spectrum[1], grad_spec[1])
    imag_out = term(spectrum[0], grad_spec[1]) - term(spectrum[1], grad_spec[0])
    return jnp.stack([real_out, imag_out])


def gelu_tanh(values):
    return jax.nn.gelu(values, approximate=True)


def shards(fields, cotangent, spectral_weight, pointwise_weight):
    groups = lax.axis_size("gz")
    depth_here = fields.shape[1]
    width_x = fields.shape[3]
    width_y = fields.shape[4]
    depth_all = depth_here * groups
    first = lax.axis_index("gz") * depth_here
    total_modes = M * M * M
    scale = 1.0 / math.sqrt(width_x * width_y * depth_all * total_modes)
    cells = lax.axis_size("dp") * fields.shape[0] * width_x * width_y * depth_all
    cos_x, sin_x = angle_table(width_x, M, 0, width_x)
    cos_y, sin_y = angle_table(width_y, M, 0, width_y)
    cos_near, sin_near = angle_table(depth_all, M, first, depth_here)
    weight = spectral_weight.astype(jnp.float32)
    inputs = fields.astype(jnp.float32)
    planes = plane_forward(inputs, cos_x, sin_x, cos_y, sin_y)
    partial_value = depth_forward(planes, cos_near, sin_near)
    input_spec = lax.psum_scatter(partial_value, "gz", scatter_dimension=3, tiled=True)
    mixed = mix_modes(input_spec, weight)
    whole = lax.all_gather(mixed, "gz", axis=3, tiled=True)
    back_planes = depth_inverse(whole, cos_near, sin_near)
    spectral = plane_inverse(back_planes, cos_x, sin_x, cos_y, sin_y) * scale
    pointwise = jnp.einsum(
        "szcxy,co->szoxy", fields, pointwise_weight, preferred_element_type=jnp.float32
    )
    pre = spectral + pointwise
    activation, pullback = jax.vjp(gelu_tanh, pre)
    grad_pre = pullback(cotangent.astype(jnp.float32))[0]
    grad_planes = plane_forward(grad_pre, cos_x, sin_x, cos_y, sin_y)
    grad_partial = depth_forward(grad_planes, cos_near, sin_near)
    grad_spec = lax.psum_scatter(grad_partial, "gz", scatter_dimension=3, tiled=True) * scale
    adjoint = mix_adjoint(grad_spec, weight)
    adjoint_whole = lax.all_gather(adjoint, "gz", axis=3, tiled=True)
    adjoint_planes = depth_inverse(adjoint_whole, cos_near, sin_near)
    back = plane_inverse(adjoint_planes, cos_x, sin_x, cos_y, sin_y)
    mixing = pointwise_weight.astype(jnp.float32)
    grad_input = back + jnp.einsum("szoxy,co->szcxy", grad_pre, mixing, precision=HIGHEST)
    point_term = jnp.einsum("szcxy,szoxy->co", inputs, grad_pre, precision=HIGHEST)
    spec_term = mix_weight_grad(input_spec, grad_spec)
    point_total = lax.psum(point_term, ("dp", "gz"))
    spec_total = lax.psum(spec_term, "dp")
    pointwise_grad = point_total * (1.0 / math.sqrt(cells))
    spectral_grad = spec_total * math.sqrt(total_modes / cells)
    return (
        activation.astype(jnp.bfloat16),
        grad_input.astype(jnp.bfloat16),
        pointwise_grad,
        spectral_grad,
    )


def solution(mesh):
    placed = (
        P("dp", "gz", None, None, None),
        P("dp", "gz", None, None, None),
        P(None, None, None, "gz"),
        P(),
    )
    return jax.shard_map(
        shards,
        mesh=mesh,
        in_specs=placed,
        out_specs=(
            P("dp", "gz", None, None, None),
            P("dp", "gz", None, None, None),
            P(),
            P(None, None, None, "gz"),
        ),
        check_vma=False,
    )
```

profile of v0, /device:TPU:0, one launch (start us, length us, event | category | flops | bytes accessed | tf_op | source)
XLA Modules:
  0.0 668.2 jit_solution(1186609376743424870)
XLA Ops:
  7.3 6.2 fusion.132
  13.5 12.2 %fusion.34 = f32[1,8,16,64,64]{4,3,2,1,0:T(8,128)S(1)} fusion(f32[64,8,16,128]{3,0,2,1:T(8,128)S(1)} %fusion.132, f32[128,32]{0,1:T(8,128)S(1)} %get-tuple-element.45, f32[128,32]{0,1:T(8,128)S(1)} %get-tuple-element.44), kind=kOutput, calls=%fused_computation.57 | convolution fusion | flops 805314560 | bytes 6324224 | tf_op jit(solution)/shard_map/szcxb,xa->szcab/dot_general | solution.py:27
  38.6 3.6 convolution_add_fusion.1
  42.2 6.2 copy.34
  48.4 7.0 %stack_reshape.12 = f32[1,1,16,32768]{3,2,1,0:T(8,128)} reshape(f32[16,1024,32]{2,1,0:T(8,128)} %copy.34) | data formatting | bytes 4194304 | tf_op jit(solution)/shard_map/stack;reshape | solution.py:44
  55.4 4.6 copy.37
  60.0 7.2 %stack_reshape.13 = f32[1,1,16,32768]{3,2,1,0:T(8,128)} reshape(f32[16,1024,32]{2,1,0:T(8,128)} %copy.37) | data formatting | bytes 4194304 | tf_op jit(solution)/shard_map/stack;reshape | solution.py:44
  67.3 4.1 pad_maximum_fusion.1
  71.5 52.8 %reduce-scatter.3.cloned.1.call-done = f32[2,1,16,4096]{3,2,1,0:T(8,128)} async-done(((f32[2,1,16,32768]{3,2,1,0:T(8,128)}), f32[2,1,16,4096]{3,2,1,0:T(8,128)}) %reduce-scatter.3.cloned.1.call-update) | async-done | bytes 524304 | tf_op jit(solution)/shard_map/reduce_scatter | solution.py:129
  130.2 8.2 %fusion.32 = f32[16,8,128,128]{3,0,2,1:T(8,128)} fusion(bf16[8,16,128,128]{3,2,1,0:T(8,128)(2,1)} %bitcast.272, bf16[16,16]{1,0:T(8,128)(2,1)S(1)} %copy-done), kind=kOutput, calls=%fused_computation.52 | convolution fusion | flops 67108864 | bytes 12583424 | tf_op jit(solution)/shard_map/szcxy,co->szoxy/dot_general | solution.py:134
  138.4 37.2 %all-gather.3.cloned.1.call-done = f32[2,1,16,32768]{3,2,1,0:T(8,128)} async-done(((f32[2,1,16,4096]{3,2,1,0:T(8,128)}), f32[2,1,16,32768]{3,2,1,0:T(8,128)}) %all-gather.3.cloned.1.call-update) | async-done | bytes 4194320 | tf_op jit(solution)/shard_map/all_gather | solution.py:131
  175.6 3.9 fusion.255
  179.4 6.0 reshape.222
  185.4 9.6 %fusion.113 = f32[8,16,1024]{2,0,1:T(8,128)S(1)} fusion(f32[16,1024,32]{2,1,0:T(8,128)} %reshape.222, s32[8]{0:T(128)S(1)} %iota_add_fusion), kind=kOutput, calls=%fused_computation.149 | convolution fusion | flops 50335232 | bytes 2621472 | tf_op jit(solution)/shard_map/scpk,zk->szcp/dot_general | solution.py:54
  195.0 7.2 %fusion.124 = f32[8,16,1024]{2,0,1:T(8,128)S(1)} fusion(f32[16,1024,32]{2,1,0:T(8,128)S(1)} %copy-done.3, s32[8]{0:T(128)S(1)} %iota_add_fusion), kind=kOutput, calls=%fused_computation.160 | convolution fusion | flops 50335232 | bytes 2621472 | tf_op jit(solution)/shard_map/scpk,zk->szcp/dot_general | solution.py:54
  202.2 5.1 reshape.223
  207.3 11.2 %convolution_add_fusion.3 = f32[8,16,1024]{2,0,1:T(8,128)} fusion(f32[8,16,1024]{2,0,1:T(8,128)S(1)} %fusion.113, f32[16,1024,32]{2,1,0:T(8,128)} %reshape.223, s32[8]{0:T(128)S(1)} %iota_add_fusion), kind=kOutput, calls=%fused_computation.89 | convolution fusion | flops 50466304 | bytes 3145760 | tf_op jit(solution)/shard_map/scpk,zk->szcp/dot_general | solution.py:54
  220.3 4.9 fusion.45
  225.2 4.9 fusion.47
  230.1 9.6 %convolution_subtract_fusion.3 = f32[8,16,1024]{2,0,1:T(8,128)S(1)} fusion(f32[8,16,1024]{2,0,1:T(8,128)S(1)} %fusion.124, f32[16,1024,32]{2,1,0:T(8,128)} %reshape.223, s32[8]{0:T(128)S(1)} %iota_add_fusion), kind=kOutput, calls=%fused_computation.90 | convolution fusion | flops 50466304 | bytes 3145760 | tf_op jit(solution)/shard_map/scpk,zk->szcp/dot_general | solution.py:54
  240.4 5.3 subtract_bitcast_fusion.2
  249.2 24.6 %fusion.2 = (f32[8,16,128,128]{3,2,1,0:T(8,128)S(1)}, bf16[1,8,16,128,128]{4,3,2,1,0:T(8,128)(2,1)}) fusion(bf16[1,8,16,128,128]{4,3,2,1,0:T(8,128)(2,1)S(1)} %copy-done.12, f32[16,8,128,128]{3,0,2,1:T(8,128)} %fusion.32, f32[128,32]{0,1:T(8,128)S(1)} %get-tuple-element.45, f32[128,32]{0,1:T(8,128)S(1)} %get-tuple-element.44, ...), kind=kOutput, calls=%fused_computation.6 | convolution fusion | flops 1662001152 | bytes 29392896 | tf_op jit(solution)/shard_map/szcxb,yb->szcxy/dot_general | solution.py:73
  273.8 9.5 %fusion.131 = f32[8,16,128,64]{2,3,1,0:T(8,128)S(1)} fusion(f32[8,16,128,128]{3,2,1,0:T(8,128)S(1)} %get-tuple-element.24, f32[128,32]{0,1:T(8,128)S(1)} %get-tuple-element.45, f32[128,32]{0,1:T(8,128)S(1)} %get-tuple-element.44), kind=kOutput, calls=%fused_computation.168 | convolution fusion | flops 1610620928 | bytes 12615680 | tf_op jit(solution)/shard_map/szcxy,yb->szcxb/dot_general | solution.py:24
  283.3 12.3 %convolution_bitcast_fusion = f32[1,8,16,64,64]{4,3,2,1,0:T(8,128)S(1)} fusion(f32[8,16,128,64]{2,3,1,0:T(8,128)S(1)} %fusion.131, f32[128,32]{0,1:T(8,128)S(1)} %get-tuple-element.45, f32[128,32]{0,1:T(8,128)S(1)} %get-tuple-element.44), kind=kOutput, calls=%fused_computation.58 | convolution fusion | flops 805314560 | bytes 6324224 | tf_op jit(solution)/shard_map/szcxb,xa->szcab/dot_general | solution.py:27
  308.1 3.6 convolution_add_fusion
  311.7 6.2 copy.51
  317.9 7.0 %stack_reshape.14 = f32[1,1,16,32768]{3,2,1,0:T(8,128)} reshape(f32[16,1024,32]{2,1,0:T(8,128)} %copy.51) | data formatting | bytes 4194304 | tf_op jit(solution)/shard_map/stack;reshape | solution.py:44
  324.9 4.7 copy.54
  329.6 7.5 %stack_reshape.15 = f32[1,1,16,32768]{3,2,1,0:T(8,128)} reshape(f32[16,1024,32]{2,1,0:T(8,128)} %copy.54) | data formatting | bytes 4194304 | tf_op jit(solution)/shard_map/stack;reshape | solution.py:44
  337.1 4.1 pad_maximum_fusion.2
  341.3 48.8 %reduce-scatter.5.cloned.1.call-done = f32[2,1,16,4096]{3,2,1,0:T(8,128)} async-done(((f32[2,1,16,32768]{3,2,1,0:T(8,128)}), f32[2,1,16,4096]{3,2,1,0:T(8,128)}) %reduce-scatter.5.cloned.1.call-update) | async-done | bytes 524304 | tf_op jit(solution)/shard_map/reduce_scatter | solution.py:142
  391.3 8.0 %add_bitcast_fusion = (f32[1,16,16,4096]{3,2,1,0:T(8,128)}, f32[1,16,16,4096]{3,2,1,0:T(8,128)}, f32[4096,16]{0,1:T(8,128)S(1)}, f32[4096,16]{0,1:T(8,128)S(1)},...) fusion(f32[4096,16]{0,1:T(8,128)S(1)} %get-tuple-element.41, f32[4096,16]{0,1:T(8,128)S(1)} %get-tuple-element.40, ...), kind=kLoop, calls=%fused_computation.56 | loop fusion | flops 16515072 | bytes 14680064 | tf_op jit(solution)/shard_map/stack | solution.py:105
  400.3 22.0 %fusion.61 = f32[16,16]{0,1:T(8,128)S(1)} fusion(bf16[8,16,128,128]{3,2,1,0:T(8,128)(2,1)} %bitcast.273, f32[8,16,128,128]{3,2,1,0:T(8,128)} %copy-done.1), kind=kOutput, calls=%fused_computation.91 | convolution fusion | flops 402653184 | bytes 12583936 | tf_op jit(solution)/shard_map/szcxy,szoxy->co/dot_general | solution.py:149
  422.3 39.4 %psum.14 = f32[16,16]{0,1:T(8,128)S(1)} all-reduce(f32[16,16]{0,1:T(8,128)S(1)} %fusion.61), channel_id=1, replica_groups=mesh['dp'=4,'gz'=8] {'dp','gz'}, use_global_device_ids=true, to_apply=%region_2.3 | all-reduce | flops 256 | bytes 2048 | tf_op jit(solution)/shard_map/psum | solution.py:151
  462.4 15.1 %fusion.13 = f32[8,128,128,16]{2,3,1,0:T(8,128)} fusion(f32[8,16,128,128]{3,2,1,0:T(8,128)} %copy-done.1, bf16[16,16]{1,0:T(8,128)(2,1)S(1)} %copy-done), kind=kOutput, calls=%fused_computation.20 | convolution fusion | flops 402653184 | bytes 16777728 | tf_op jit(solution)/shard_map/szoxy,co->szcxy/dot_general | solution.py:148
  477.5 3.8 pad_maximum_fusion
  481.3 3.8 fusion.254
  485.1 6.0 reshape.233
  491.1 5.2 reshape.232
  496.3 9.9 %fusion.108 = f32[8,16,1024]{2,0,1:T(8,128)S(1)} fusion(f32[16,1024,32]{2,1,0:T(8,128)} %reshape.232, s32[8]{0:T(128)S(1)} %iota_add_fusion), kind=kOutput, calls=%fused_computation.144 | convolution fusion | flops 50335232 | bytes 2621472 | tf_op jit(solution)/shard_map/scpk,zk->szcp/dot_general | solution.py:54
  506.2 7.2 %convolution_add_fusion.2 = f32[8,16,1024]{2,0,1:T(8,128)S(1)} fusion(f32[8,16,1024]{2,0,1:T(8,128)S(1)} %fusion.108, f32[16,1024,32]{2,1,0:T(8,128)S(1)} %copy-done.2, s32[8]{0:T(128)S(1)} %iota_add_fusion), kind=kOutput, calls=%fused_computation.87 | convolution fusion | flops 50466304 | bytes 3145760 | tf_op jit(solution)/shard_map/scpk,zk->szcp/dot_general | solution.py:54
  515.5 9.8 %fusion.119 = f32[8,16,1024]{2,0,1:T(8,128)S(1)} fusion(f32[16,1024,32]{2,1,0:T(8,128)} %reshape.232, s32[8]{0:T(128)S(1)} %iota_add_fusion), kind=kOutput, calls=%fused_computation.155 | convolution fusion | flops 50335232 | bytes 2621472 | tf_op jit(solution)/shard_map/scpk,zk->szcp/dot_general | solution.py:54
  525.2 9.6 %convolution_subtract_fusion.2 = f32[8,16,1024]{2,0,1:T(8,128)S(1)} fusion(f32[8,16,1024]{2,0,1:T(8,128)S(1)} %fusion.119, f32[16,1024,32]{2,1,0:T(8,128)} %reshape.233, s32[8]{0:T(128)S(1)} %iota_add_fusion), kind=kOutput, calls=%fused_computation.88 | convolution fusion | flops 50466304 | bytes 3145760 | tf_op jit(solution)/shard_map/scpk,zk->szcp/dot_general | solution.py:54
  535.5 5.0 fusion.39
  547.6 3.8 add_bitcast_fusion.1
  551.4 17.5 %fusion.10 = bf16[1,8,16,128,128]{4,3,2,1,0:T(8,128)(2,1)} fusion(f32[8,128,128,16]{2,3,1,0:T(8,128)S(1)} %bitcast.275, f32[1,8,16,128,32]{3,4,2,1,0:T(8,128)S(1)} %add_bitcast_fusion.1, f32[1,8,16,128,32]{3,4,2,1,0:T(8,128)S(1)} %subtract_bitcast_fusion.1, f32[128,32]{0,1:T(8,128)S(1)} %get-tuple-element.45, f32[128,32]{0,1:T(8,128)S(1)} %get-tuple-element.44), kind=kOutput, calls=%fused_computation.16 | convolution fusion | flops 1615863808 | bytes 16809984 | tf_op jit(solution)/shard_map/szcxb,yb->szcxy/dot_general | solution.py:73
  568.9 84.3 %all-reduce.2.cloned.1.call-done = f32[2,16,16,4096]{3,2,1,0:T(8,128)} async-done(((f32[2,16,16,4096]{3,2,1,0:T(8,128)}), f32[2,16,16,4096]{3,2,1,0:T(8,128)}) %all-reduce.2.cloned.1.call-update) | async-done | bytes 8388624 | tf_op jit(solution)/shard_map/psum | solution.py:152
  653.1 8.3 %broadcast_multiply_fusion = f32[2,16,16,4096]{3,2,1,0:T(8,128)} fusion(f32[2,16,16,4096]{3,2,1,0:T(8,128)} %all-reduce.2.cloned.1.call-done), kind=kLoop, calls=%fused_computation.54 | loop fusion | flops 2097152 | bytes 16777216 | tf_op jit(solution)/shard_map/mul | solution.py:154
  (75 shorter events, 50.0 us)
Async XLA Ops:
  7.2 123.0 %copy-start = (bf16[16,16]{1,0:T(8,128)(2,1)S(1)}, bf16[16,16]{1,0:T(8,128)(2,1)}, u32[]{:S(2)}) copy-start(bf16[16,16]{1,0:T(8,128)(2,1)} %param.7) | copy-start | bytes 1540
  7.2 117.1 %reduce-scatter.3.cloned.1.call-start = ((), (), s32[]{:S(2)}) async-start(), calls=%async_computation.2 | async-start | bytes 4718592 | tf_op jit(solution)/shard_map/reduce_scatter | solution.py:129
  60.0 7.3 %copy-start.8 = (f32[1,1,16,32768]{3,2,1,0:T(8,128)S(1)}, f32[1,1,16,32768]{3,2,1,0:T(8,128)}, u32[]{:S(2)}) copy-start(f32[1,1,16,32768]{3,2,1,0:T(8,128)} %stack_reshape.12) | copy-start | bytes 6291460
  71.5 104.1 %all-gather.3.cloned.1.call-start = ((), (), s32[]{:S(2)}) async-start(), calls=%async_computation.3 | async-start | bytes 4718592 | tf_op jit(solution)/shard_map/all_gather | solution.py:131
  125.4 0.7 copy-start.10
  130.1 260.1 %reduce-scatter.5.cloned.1.call-start = ((), (), s32[]{:S(2)}) async-start(), calls=%async_computation.4 | async-start | bytes 4718592 | tf_op jit(solution)/shard_map/reduce_scatter | solution.py:142
  185.4 9.6 %copy-start.3 = (f32[16,1024,32]{2,1,0:T(8,128)S(1)}, f32[16,1024,32]{2,1,0:T(8,128)}, u32[]{:S(2)}) copy-start(f32[16,1024,32]{2,1,0:T(8,128)} %reshape.222) | copy-start | bytes 6291460
  240.4 5.3 copy-start.7
  245.7 3.6 copy-start.12
  273.8 9.5 %copy-start.1 = (f32[8,16,128,128]{3,2,1,0:T(8,128)}, f32[8,16,128,128]{3,2,1,0:T(8,128)S(1)}, u32[]{:S(2)}) copy-start(f32[8,16,128,128]{3,2,1,0:T(8,128)S(1)} %get-tuple-element.24) | copy-start | bytes 25165828
  329.6 7.6 %copy-start.9 = (f32[1,1,16,32768]{3,2,1,0:T(8,128)S(1)}, f32[1,1,16,32768]{3,2,1,0:T(8,128)}, u32[]{:S(2)}) copy-start(f32[1,1,16,32768]{3,2,1,0:T(8,128)} %stack_reshape.14) | copy-start | bytes 6291460
  341.3 50.0 %copy-start.11 = (f32[4096,16]{0,1:T(8,128)S(1)}, f32[4096,16]{0,1:T(8,128)}, u32[]{:S(2)}) copy-start(f32[4096,16]{0,1:T(8,128)} %copy-done.10) | copy-start | bytes 786436
  341.3 140.0 %all-gather.5.cloned.1.call-start = ((), (), s32[]{:S(2)}) async-start(), calls=%async_computation.5 | async-start | bytes 4718592 | tf_op jit(solution)/shard_map/all_gather | solution.py:144
  400.2 252.9 %all-reduce.2.cloned.1.call-start = ((), (), s32[]{:S(2)}) async-start(), calls=%async_computation.6 | async-start | bytes 16777216 | tf_op jit(solution)/shard_map/psum | solution.py:152
  462.4 15.1 %copy-start.5 = (f32[1,16,16,4096]{3,2,1,0:T(8,128)S(1)}, f32[1,16,16,4096]{3,2,1,0:T(8,128)}, u32[]{:S(2)}) copy-start(f32[1,16,16,4096]{3,2,1,0:T(8,128)} %get-tuple-element.34) | copy-start | bytes 12582916
  462.4 15.1 %copy-start.6 = (f32[1,16,16,4096]{3,2,1,0:T(8,128)S(1)}, f32[1,16,16,4096]{3,2,1,0:T(8,128)}, u32[]{:S(2)}) copy-start(f32[1,16,16,4096]{3,2,1,0:T(8,128)} %get-tuple-element.35) | copy-start | bytes 12582916
  496.3 9.9 %copy-start.2 = (f32[16,1024,32]{2,1,0:T(8,128)S(1)}, f32[16,1024,32]{2,1,0:T(8,128)}, u32[]{:S(2)}) copy-start(f32[16,1024,32]{2,1,0:T(8,128)} %reshape.233) | copy-start | bytes 6291460
  540.6 3.6 copy-start.4
  540.6 10.8 %slice-start = ((s8[8388608]{0:T(1024)(128)(4,1)}), s8[4194304]{0:T(1024)(128)(4,1)S(1)}, s32[]{:S(2)}) async-start(s8[8388608]{0:T(1024)(128)(4,1)} %bitcast.274), calls=%async_computation.7 | async-start | bytes 8388608
  544.2 7.2 %slice-start.1 = ((s8[8388608]{0:T(1024)(128)(4,1)}), s8[4194304]{0:T(1024)(128)(4,1)S(1)}, s32[]{:S(2)}) async-start(s8[8388608]{0:T(1024)(128)(4,1)} %bitcast.274), calls=%async_computation.8 | async-start | bytes 8388608
Sparse Core Ops, SparseCore 0:
  71.6 52.6 reduce-scatter.2
  130.2 45.2 all-gather.2
  341.4 48.7 reduce-scatter.4
  400.4 45.7 all-gather.4
  481.4 171.6 all-reduce.1
where the time goes:
time: 677 us; the launch traced here: 668 us
  matrix products  256 us (38%)
  waiting for transfers between devices  223 us (33%)
  local copies, waits for them, and re-layouts  95.3 us (14%)
  blocking collectives  39.4 us (6%)
  other arithmetic  39.3 us (6%)
  between operations  14.4 us (2%)
    psum x1, waiting for transfers between devices, shards(): spec_total = lax.psum(spec_term, 'dp')  84.3 us
    dot_general x8, matrix products, expand(): return jnp.einsum('scpk,zk->szcp', values, table, precision=HIGHEST)  74.2 us
    reduce_scatter x1, waiting for transfers between devices, shards(): lax.psum_scatter(partial_value, 'gz', scatter_dimension=3, tiled=True)  52.8 us
    reduce_scatter x1, waiting for transfers between devices, shards(): lax.psum_scatter(grad_partial, 'gz', scatter_dimension=3, tiled=True)  48.8 us
    dot_general x2, matrix products, plane_inverse(): jnp.einsum('szcxb,yb->szcxy', joined, jnp.concatenate([cos_y, -sin_y], ax...  42 us
    psum x1, blocking collectives, shards(): point_total = lax.psum(point_term, ('dp', 'gz'))  39.4 us
    all_gather x1, waiting for transfers between devices, shards(): whole = lax.all_gather(mixed, 'gz', axis=3, tiled=True)  37.2 us
    another operation x12, local copies, waits for them, and re-layouts  34.6 us
  transfers between devices with their start and end apart: 5, of which 4 were waited for; matrix products, arithmetic and copies ran while one was open for 21% of the time, Pallas kernels for 0%

commit v1 on v0

v1 whole, which is shorter than its diff:
```python
import functools
import math

import jax
import jax.numpy as jnp
import ml_dtypes
import numpy as np
from jax import lax
from jax.experimental import pallas as pl
from jax.experimental.pallas import tpu as pltpu
from jax.sharding import PartitionSpec as P

M = 32
QUAD = 4
F32 = jnp.float32
BF16 = jnp.bfloat16
NN = (((1,), (0,)), ((), ()))
TN = (((0,), (0,)), ((), ()))
NT = (((1,), (1,)), ((), ()))
GELU_A = math.sqrt(2.0 / math.pi)
GELU_B = 0.044715


def halves(table):
    high = table.astype(np.float32).astype(ml_dtypes.bfloat16)
    low = (table - high.astype(np.float64)).astype(np.float32).astype(ml_dtypes.bfloat16)
    return high, low


def trig(length, modes):
    phase = np.outer(np.arange(length), modes) % length
    angles = phase * (2.0 * math.pi / length)
    return np.cos(angles), np.sin(angles)


def complex_block(cos, sin, sign):
    return np.array([[cos, sign * sin], [-sign * sin, cos]])


def tables(width_x, width_y, depth, owned_x):
    order_y = (np.arange(M) % (M // QUAD)) * QUAD + np.arange(M) // (M // QUAD)
    cos_x, sin_x = trig(width_x, np.arange(M))
    cos_y, sin_y = trig(width_y, order_y)
    cos_z, sin_z = trig(depth, np.arange(M))
    eye4 = np.eye(QUAD)
    eye_a = np.eye(owned_x)
    y_fwd = np.einsum("pq,ryb->pyrqb", eye4, np.array([cos_y, -sin_y]))
    y_fwd = y_fwd.reshape(QUAD * width_y, 2 * QUAD * M)
    y_inv = np.einsum("pq,ryb->rpbqy", eye4, np.array([cos_y, -sin_y]))
    y_inv = y_inv.reshape(2 * QUAD * M, QUAD * width_y)
    x_fwd = np.einsum("ijxa->ajix", complex_block(cos_x, sin_x, -1.0)).reshape(2 * M, 2 * width_x)
    x_inv = np.einsum("ijxa->jxai", complex_block(cos_x, sin_x, 1.0)).reshape(2 * width_x, 2 * M)
    ones = np.ones(QUAD)
    z_fwd = np.einsum("ac,ijzk,r->zaicjrk", eye_a, complex_block(cos_z, sin_z, -1.0), ones)
    z_fwd = z_fwd.reshape(depth * owned_x * 2, owned_x * 2 * QUAD * M)
    z_inv = np.einsum("ac,ijzk,r->zcjairk", eye_a, complex_block(cos_z, sin_z, 1.0), ones)
    z_inv = z_inv.reshape(depth * owned_x * 2, owned_x * 2 * QUAD * M)
    xi_h, xi_l = halves(x_inv)
    x_inv4 = np.concatenate([xi_h, xi_l, xi_h, xi_l], axis=1)
    x_fwd2 = np.concatenate(halves(x_fwd), axis=0)
    return dict(
        y_fwd=np.stack(halves(y_fwd)),
        y_inv=np.stack(halves(y_inv)),
        x_fwd=x_fwd2,
        x_inv=x_inv4,
        z_fwd=np.stack(halves(z_fwd)),
        z_inv=np.stack(halves(z_inv)),
    )


def split(values):
    high = values.astype(BF16)
    return high, (values - high.astype(F32)).astype(BF16)


def dot(left, right, dims=NN):
    return lax.dot_general(left, right, dims, preferred_element_type=F32)


def x_forward(real, imag, x_fwd_ref):
    high, low = split(jnp.concatenate([real, imag], axis=0))
    both = dot(x_fwd_ref[...], high)
    rows = both.shape[0] // 2
    return both[:rows] + both[rows:] + dot(x_fwd_ref[:rows], low)


def store_blocks(out_ref, values):
    groups, rows = out_ref.shape[0], out_ref.shape[2]
    for d in range(groups):
        out_ref[d, 0] = values[d * rows:(d + 1) * rows]


def load_blocks(in_ref, scratch):
    groups, rows = in_ref.shape[0], in_ref.shape[2]
    if rows % 8 == 0:
        return in_ref[:, 0].reshape(groups * rows, in_ref.shape[3])
    for d in range(groups):
        scratch[d * rows:(d + 1) * rows] = in_ref[d, 0]
    return scratch[...]


def fields_kernel(f_ref, y_fwd_ref, x_fwd_ref, out_ref):
    channels = f_ref.shape[2]
    real, imag = [], []
    for j in range(channels // QUAD):
        planes = jnp.concatenate([f_ref[0, 0, QUAD * j + p] for p in range(QUAD)], axis=1)
        g = dot(planes, y_fwd_ref[0]) + dot(planes, y_fwd_ref[1])
        half = g.shape[1] // 2
        real.append(g[:, :half])
        imag.append(g[:, half:])
    values = x_forward(jnp.concatenate(real, axis=1), jnp.concatenate(imag, axis=1), x_fwd_ref)
    store_blocks(out_ref, values)


def inverse_planes(p, x_inv_ref, y_inv_ref):
    high, low = split(p)
    q = dot(x_inv_ref[...], jnp.concatenate([high, high, low, low], axis=0))
    q_high, q_low = split(q)
    rows = q.shape[0] // 2
    wide = QUAD * M
    for j in range(q.shape[1] // wide):
        here = slice(j * wide, (j + 1) * wide)
        left_high = jnp.concatenate([q_high[:rows, here], q_high[rows:, here]], axis=1)
        left_low = jnp.concatenate([q_low[:rows, here], q_low[rows:, here]], axis=1)
        yield j, (
            dot(left_high, y_inv_ref[0]) + dot(left_high, y_inv_ref[1]) + dot(left_low, y_inv_ref[0])
        )


def middle_kernel(p_ref, f_ref, cot_ref, w1_ref, w2_ref, y_fwd_ref, x_fwd_ref, y_inv_ref, x_inv_ref,
                  act_ref, part_ref, out_ref, pg_ref, p_scr, spec, g_high, g_low):
    channels, width_x, width_y = f_ref.shape[2:]
    group = 16

    @pl.when(pl.program_id(0) == 0)
    def _():
        pg_ref[...] = jnp.zeros_like(pg_ref)

    for j, value in inverse_planes(load_blocks(p_ref, p_scr), x_inv_ref, y_inv_ref):
        for p in range(QUAD):
            spec[QUAD * j + p] = value[:, p * width_y:(p + 1) * width_y]

    rows = channels * group

    def step(t, carry):
        first = pl.multiple_of(t * 2 * group, 2 * group)
        cells = [pl.ds(first, group), pl.ds(first + group, group)]

        def both(read):
            return jnp.concatenate([read(s).reshape(rows, width_y) for s in cells], axis=1)

        f = both(lambda s: f_ref[0, 0, :, s, :])
        pre = dot(w1_ref[...], f) + both(lambda s: spec[:, s, :])
        square = pre * pre
        t_val = jnp.tanh(GELU_A * pre * (1.0 + GELU_B * square))
        cdf = 0.5 + 0.5 * t_val
        act = (pre * cdf).astype(BF16)
        slope = cdf + pre * (0.5 - 0.5 * t_val * t_val) * (GELU_A + 3.0 * GELU_A * GELU_B * square)
        g = both(lambda s: cot_ref[0, 0, :, s, :]).astype(F32) * slope
        high, low = split(g)
        part = dot(w2_ref[...], high) + dot(w2_ref[...], low)
        pg = None
        for i, s in enumerate(cells):
            lanes = slice(i * width_y, (i + 1) * width_y)
            shape = (channels, group, width_y)
            act_ref[0, 0, :, s, :] = act[:, lanes].reshape(shape)
            part_ref[0, :, s, :] = part[:, lanes].reshape(shape)
            g_high[:, s, :] = high[:, lanes].reshape(shape)
            g_low[:, s, :] = low[:, lanes].reshape(shape)
        pg_ref[...] += dot(f, high, NT) + dot(f, low, NT)
        return carry

    lax.fori_loop(0, width_x // (2 * group), step, 0)

    real, imag = [], []
    for j in range(channels // QUAD):
        planes = [jnp.concatenate([r[QUAD * j + p] for p in range(QUAD)], axis=1) for r in (g_high, g_low)]
        v = dot(planes[0], y_fwd_ref[0]) + dot(planes[0], y_fwd_ref[1]) + dot(planes[1], y_fwd_ref[0])
        half = v.shape[1] // 2
        real.append(v[:, :half])
        imag.append(v[:, half:])
    values = x_forward(jnp.concatenate(real, axis=1), jnp.concatenate(imag, axis=1), x_fwd_ref)
    store_blocks(out_ref, values)


def final_kernel(p_ref, part_ref, y_inv_ref, x_inv_ref, out_ref, p_scr):
    width_y = out_ref.shape[4]
    for j, value in inverse_planes(load_blocks(p_ref, p_scr), x_inv_ref, y_inv_ref):
        for p in range(QUAD):
            c = QUAD * j + p
            out_ref[0, 0, c] = (value[:, p * width_y:(p + 1) * width_y] + part_ref[0, c]).astype(BF16)


def lane_quad(shape):
    return lax.broadcasted_iota(jnp.int32, shape, len(shape) - 1) // M


def depth_forward(s_ref, z_fwd_ref, spec_ref, scale):
    high, low = split(s_ref[...])
    v = dot(high, z_fwd_ref[0], TN) + dot(high, z_fwd_ref[1], TN) + dot(low, z_fwd_ref[0], TN)
    tall = M // QUAD
    wide = QUAD * M
    channels = v.shape[0] // M
    v = v.reshape(channels, QUAD, tall, v.shape[1])
    quad = lane_quad((channels, tall, wide))
    for a in range(v.shape[3] // (2 * wide)):
        for part in range(2):
            lanes = slice((2 * a + part) * wide, (2 * a + part + 1) * wide)
            u = v[:, 0, :, lanes]
            for r in range(1, QUAD):
                u = jnp.where(quad == r, v[:, r, :, lanes], u)
            spec_ref[part, :, a * tall:(a + 1) * tall, :] = u * scale if scale != 1.0 else u


def depth_inverse(spec_ref, z_inv_ref, out_ref):
    channels, places, wide = spec_ref.shape[1:]
    tall = M // QUAD
    quad = lane_quad((channels, tall, wide))
    pieces = []
    for a in range(places // tall):
        for part in range(2):
            v = spec_ref[part, :, a * tall:(a + 1) * tall, :]
            masked = jnp.stack([jnp.where(quad == r, v, 0.0) for r in range(QUAD)], axis=1)
            pieces.append(masked.reshape(channels * M, wide))
    high, low = split(jnp.concatenate(pieces, axis=1))
    out_ref[...] = dot(z_inv_ref[0], high, NT) + dot(z_inv_ref[1], high, NT) + dot(z_inv_ref[0], low, NT)


def mix_kernel(scale, s_ref, r_ref, z_fwd_ref, z_inv_ref, out_ref, u_ref, v_scr):
    channels, places, wide = u_ref.shape[1:]
    depth_forward(s_ref, z_fwd_ref, u_ref, 1.0)

    def step(q, carry):
        lanes = pl.ds(pl.multiple_of(q * wide, wide), wide)
        real = jnp.zeros((channels, wide), F32)
        imag = jnp.zeros((channels, wide), F32)
        for c in range(channels):
            w_re = r_ref[0, c, :, lanes].astype(F32)
            w_im = r_ref[1, c, :, lanes].astype(F32)
            u_re = u_ref[0, c, pl.ds(q, 1), :]
            u_im = u_ref[1, c, pl.ds(q, 1), :]
            real += u_re * w_re - u_im * w_im
            imag += u_re * w_im + u_im * w_re
        v_scr[0, :, pl.ds(q, 1), :] = (real * scale)[:, None, :]
        v_scr[1, :, pl.ds(q, 1), :] = (imag * scale)[:, None, :]
        return carry

    lax.fori_loop(0, places, step, 0)
    depth_inverse(v_scr, z_inv_ref, out_ref)


def adjoint_kernel(scale, s_ref, r_ref, z_fwd_ref, z_inv_ref, out_ref, dv_ref, du_scr):
    channels, places, wide = dv_ref.shape[1:]
    depth_forward(s_ref, z_fwd_ref, dv_ref, scale)

    def step(q, carry):
        lanes = pl.ds(pl.multiple_of(q * wide, wide), wide)
        d_re = dv_ref[0, :, pl.ds(q, 1), :].reshape(channels, wide)
        d_im = dv_ref[1, :, pl.ds(q, 1), :].reshape(channels, wide)
        for c in range(channels):
            w_re = r_ref[0, c, :, lanes].astype(F32)
            w_im = r_ref[1, c, :, lanes].astype(F32)
            du_scr[0, c, pl.ds(q, 1), :] = jnp.sum(d_re * w_re + d_im * w_im, axis=0, keepdims=True)
            du_scr[1, c, pl.ds(q, 1), :] = jnp.sum(d_im * w_re - d_re * w_im, axis=0, keepdims=True)
        return carry

    lax.fori_loop(0, places, step, 0)
    depth_inverse(du_scr, z_inv_ref, out_ref)


def weight_grad_kernel(scale, *refs):
    count = (len(refs) - 1) // 2
    u_refs, dv_refs, out_ref = refs[:count], refs[count:2 * count], refs[-1]
    channels, places, wide = u_refs[0].shape[1:]
    for q in range(places):
        lanes = slice(q * wide, (q + 1) * wide)
        dv = [[r[part, :, q, :] * scale for part in range(2)] for r in dv_refs]
        for c in range(channels):
            real = imag = None
            for s in range(count):
                u_re = u_refs[s][0, c, q:q + 1, :]
                u_im = u_refs[s][1, c, q:q + 1, :]
                d_re, d_im = dv[s]
                t_re = u_re * d_re + u_im * d_im
                t_im = u_re * d_im - u_im * d_re
                real = t_re if real is None else real + t_re
                imag = t_im if imag is None else imag + t_im
            out_ref[0, c, :, lanes] = real
            out_ref[1, c, :, lanes] = imag


def params(steps, megabytes=48):
    return pltpu.CompilerParams(
        dimension_semantics=("arbitrary",) * steps, vmem_limit_bytes=megabytes * 1024 * 1024
    )


def whole_spec(array):
    rank = len(array.shape)
    return pl.BlockSpec(tuple(array.shape), lambda *i: (0,) * rank)


def shards(fields, cotangent, spectral_weight, pointwise_weight):
    groups = lax.axis_size("gz")
    samples = lax.axis_size("dp")
    _, near, channels, width_x, width_y = fields.shape
    depth = near * groups
    owned = M // groups
    rows = 2 * owned
    wide = channels * M
    places = spectral_weight.shape[3] // (QUAD * M)
    total_modes = M * M * M
    cells = samples * width_x * width_y * depth
    scale = 1.0 / math.sqrt(width_x * width_y * depth * total_modes)
    tab = {k: jnp.asarray(v) for k, v in tables(width_x, width_y, depth, owned).items()}

    plane = pl.BlockSpec((1, 1, channels, width_x, width_y), lambda z: (0, z, 0, 0, 0))
    part_spec = pl.BlockSpec((1, channels, width_x, width_y), lambda z: (z, 0, 0, 0))
    block = pl.BlockSpec((groups, 1, rows, wide), lambda z: (0, z, 0, 0))
    block_shape = jax.ShapeDtypeStruct((groups, near, rows, wide), F32)
    spec_shape = jax.ShapeDtypeStruct((2, channels, places, QUAD * M), F32)
    out_field = jax.ShapeDtypeStruct(fields.shape, BF16)
    flat = (depth * rows, wide)

    def exchange(values):
        return lax.all_to_all(values, "gz", 0, 0, tiled=True)

    def gather(values):
        pieces = [values]
        for k in range(1, samples):
            pieces.append(lax.ppermute(values, "dp", [(i, i ^ k) for i in range(samples)]))
        return pieces

    forward = pl.pallas_call(
        fields_kernel,
        grid=(near,),
        in_specs=[plane, whole_spec(tab["y_fwd"]), whole_spec(tab["x_fwd"])],
        out_specs=block,
        out_shape=block_shape,
        compiler_params=params(1),
        name="fields_forward",
    )(fields, tab["y_fwd"], tab["x_fwd"])
    arrived = exchange(forward).reshape(flat)

    mixed, u_spec = pl.pallas_call(
        functools.partial(mix_kernel, scale),
        out_shape=(jax.ShapeDtypeStruct(flat, F32), spec_shape),
        scratch_shapes=[pltpu.VMEM(spec_shape.shape, F32)],
        compiler_params=params(0),
        name="mix_modes",
    )(arrived, spectral_weight, tab["z_fwd"], tab["z_inv"])
    u_all = gather(u_spec)
    planes = exchange(mixed.reshape(block_shape.shape))

    eye = jnp.eye(16, dtype=BF16)
    weight1 = jnp.kron(pointwise_weight.T, eye)
    weight2 = jnp.kron(pointwise_weight, eye)
    side = channels * 16
    scratch_planes = (channels, width_x, width_y)
    layer_output, part, grad_forward, point = pl.pallas_call(
        middle_kernel,
        grid=(near,),
        in_specs=[block, plane, plane, whole_spec(weight1), whole_spec(weight2), whole_spec(tab["y_fwd"]),
                  whole_spec(tab["x_fwd"]), whole_spec(tab["y_inv"]), whole_spec(tab["x_inv"])],
        out_specs=[plane, part_spec, block, pl.BlockSpec((side, side), lambda z: (0, 0))],
        out_shape=[out_field, jax.ShapeDtypeStruct((near, *scratch_planes), F32), block_shape,
                   jax.ShapeDtypeStruct((side, side), F32)],
        scratch_shapes=[pltpu.VMEM((2 * M, wide), F32), pltpu.VMEM(scratch_planes, F32),
                        pltpu.VMEM(scratch_planes, BF16), pltpu.VMEM(scratch_planes, BF16)],
        compiler_params=params(1),
        name="middle",
    )(planes, fields, cotangent, weight1, weight2, tab["y_fwd"], tab["x_fwd"], tab["y_inv"], tab["x_inv"])

    arrived = exchange(grad_forward).reshape(flat)
    adjoint, dv_spec = pl.pallas_call(
        functools.partial(adjoint_kernel, scale),
        out_shape=(jax.ShapeDtypeStruct(flat, F32), spec_shape),
        scratch_shapes=[pltpu.VMEM(spec_shape.shape, F32)],
        compiler_params=params(0),
        name="mix_adjoint",
    )(arrived, spectral_weight, tab["z_fwd"], tab["z_inv"])
    dv_all = gather(dv_spec)
    planes = exchange(adjoint.reshape(block_shape.shape))

    input_grad = pl.pallas_call(
        final_kernel,
        grid=(near,),
        in_specs=[block, part_spec, whole_spec(tab["y_inv"]), whole_spec(tab["x_inv"])],
        out_specs=plane,
        out_shape=out_field,
        scratch_shapes=[pltpu.VMEM((2 * M, wide), F32)],
        compiler_params=params(1),
        name="input_gradient",
    )(planes, part, tab["y_inv"], tab["x_inv"])

    tall = 8
    spec_block = pl.BlockSpec((2, channels, tall, QUAD * M), lambda q: (0, 0, q, 0))
    spectral_grad = pl.pallas_call(
        functools.partial(weight_grad_kernel, math.sqrt(total_modes / cells)),
        grid=(places // tall,),
        in_specs=[spec_block] * (2 * samples),
        out_specs=pl.BlockSpec((2, channels, channels, tall * QUAD * M), lambda q: (0, 0, 0, q)),
        out_shape=jax.ShapeDtypeStruct(spectral_weight.shape, F32),
        compiler_params=params(1),
        name="weight_gradient",
    )(*u_all, *dv_all)

    point = jnp.einsum("cxox->co", point.reshape(channels, 16, channels, 16))
    pointwise_grad = lax.psum(point, ("dp", "gz")) * (1.0 / math.sqrt(cells))
    return layer_output, input_grad, pointwise_grad, spectral_grad


def solution(mesh):
    placed = (
        P("dp", "gz", None, None, None),
        P("dp", "gz", None, None, None),
        P(None, None, None, "gz"),
        P(),
    )
    return jax.shard_map(
        shards,
        mesh=mesh,
        in_specs=placed,
        out_specs=(
            P("dp", "gz", None, None, None),
            P("dp", "gz", None, None, None),
            P(),
            P(None, None, None, "gz"),
        ),
        check_vma=False,
    )
```

time: 677 us -> 269 us (0.40); the launches traced: 668 us -> 268 us
  matrix products: 256 us -> 0 us
  waiting for transfers between devices: 223 us -> 29.7 us
  blocking collectives: 39.4 us -> 123 us
  local copies, waits for them, and re-layouts: 95.3 us -> 16.3 us
  Pallas kernels: 0 us -> 78.7 us
  other arithmetic: 39.3 us -> 4.01 us
  starting transfers between devices: 0.21 us -> 15.2 us
  between operations: 14.4 us -> 0.77 us
    dot_general x33 -> x0, matrix products: 256 us -> none  [the longest x8 74.2 us: expand(): return jnp.einsum('scpk,zk->szcp', values, table, precision=HIGHEST)]
    reduce_scatter x2 -> x0, waiting for transfers between devices: 102 us -> none  [the longest x1 52.8 us: shards(): lax.psum_scatter(partial_value, 'gz', scatter_dimension=3, tiled=True)]
    psum x1 -> x0, waiting for transfers between devices: 84.3 us -> none  [shards(): spec_total = lax.psum(spec_term, 'dp')]
    pallas_call x0 -> x6, Pallas kernels: none -> 78.7 us  [the longest x1 35.5 us: shards(): pl.pallas_call(middle_kernel, grid=(near,), in_specs=[block, plane, plane...]
    another operation x16 -> x0, local copies, waits for them, and re-layouts: 63.4 us -> none
    all_to_all x0 -> x2, blocking collectives: none -> 61.7 us  [exchange(): return lax.all_to_all(values, 'gz', 0, 0, tiled=True)]
    all_gather x2 -> x0, waiting for transfers between devices: 37.2 us -> none  [the longest x1 37.2 us: shards(): whole = lax.all_gather(mixed, 'gz', axis=3, tiled=True)]
    psum x1, blocking collectives: 39.4 us -> 61.5 us  [shards(): pointwise_grad = lax.psum(point, ('dp', 'gz')) * (1.0 / math.sqrt(cells))]
  transfers between devices with their start and end apart: 5 -> 8, of which waited for: 4 -> 2; matrix products, arithmetic and copies ran while one was open for 21% -> 4% of each run, Pallas kernels for 0% -> 3%
where the time goes in v1:
time: 269 us; the launch traced here: 268 us
  blocking collectives  123 us (46%)
  Pallas kernels  78.7 us (29%)
  waiting for transfers between devices  29.7 us (11%)
  local copies, waits for them, and re-layouts  16.3 us (6%)
  starting transfers between devices  15.2 us (6%)
  other arithmetic  4.01 us (1%)
    all_to_all x2, blocking collectives, exchange(): return lax.all_to_all(values, 'gz', 0, 0, tiled=True)  61.7 us
    psum x1, blocking collectives, shards(): pointwise_grad = lax.psum(point, ('dp', 'gz')) * (1.0 / math.sqrt(cells))  61.5 us
    pallas_call x1, Pallas kernels, shards(): pl.pallas_call(middle_kernel, grid=(near,), in_specs=[block, plane, plane...  35.5 us
    all_to_all x2, waiting for transfers between devices, exchange(): return lax.all_to_all(values, 'gz', 0, 0, tiled=True)  20.4 us
    pallas_call x1, Pallas kernels, shards(): pl.pallas_call(final_kernel, grid=(near,), in_specs=[block, part_spec, wh...  10.3 us
    pallas_call x1, Pallas kernels, shards(): pl.pallas_call(functools.partial(adjoint_kernel, scale), out_shape=(jax.S...  9.85 us
    ppermute x6, waiting for transfers between devices, gather(): lax.ppermute(values, 'dp', [(i, i ^ k) for i in range(samples)])  9.27 us
    pallas_call x1, Pallas kernels, shards(): pl.pallas_call(functools.partial(weight_grad_kernel, math.sqrt(total_mode...  9.14 us
  transfers between devices with their start and end apart: 8, of which 2 were waited for; matrix products, arithmetic and copies ran while one was open for 4% of the time, Pallas kernels for 3%

profile of v1, /device:TPU:0, one launch (start us, length us, event | category | flops | bytes accessed | tf_op | source)
XLA Modules:
  0.0 267.9 jit_solution(13411928491181315291)
XLA Ops:
  0.6 0.0 copy-start
  0.6 0.0 copy-start.1
  0.7 2.3 copy-done.1
  3.0 1.0 copy-done.4
  4.0 0.8 copy-done.10
  4.9 5.2 %fields_forward.1 = f32[8,8,8,512]{3,2,1,0:T(8,128)S(1)} custom-call(bf16[1,8,16,128,128]{4,3,2,1,0:T(8,128)(2,1)S(1)} %copy-done.1, bf16[2,512,256]{2,1,0:T(8,128)(2,1)S(1)} %copy-done.4, bf16[128,256]{1,0:T(8,128)(2,1)S(1)} %copy-done.10), custom_call_target="tpu_custom_call" | custom-call | tf_op jit(solution)/shard_map/fields_forward/pallas_call | solution.py:334
  10.1 32.7 %all_to_all.20 = f32[8,8,8,512]{3,2,1,0:T(8,128)S(1)} all-to-all(f32[8,8,8,512]{3,2,1,0:T(8,128)S(1)} %fields_forward.1), channel_id=1, replica_groups=mesh['dp'=4,'gz'=8] {'gz'}, dimensions={0} | all-to-all | bytes 2097152 | tf_op jit(solution)/shard_map/all_to_all | solution.py:326
  42.8 0.0 copy-done
  42.8 8.7 %mix_modes.1 = (f32[512,512]{1,0:T(8,128)S(1)}, f32[2,16,32,128]{3,2,1,0:T(8,128)S(1)}) custom-call(f32[512,512]{1,0:T(8,128)S(1)} %bitcast.10, bf16[2,16,16,4096]{3,2,1,0:T(8,128)(2,1)} %r_ref.3, bf16[2,512,1024]{2,1,0:T(8,128)(2,1)S(1)} %copy-done, bf16[2,512,1024]{2,1,0:T(8,128)(2,1)S(1)} %copy-done), custom_call_target="tpu_custom_call" | custom-call | tf_op jit(solution)/shard_map/mix_modes/pallas_call | solution.py:345
  51.5 0.0 copy-start.6
  51.5 1.0 copy-done.6
  52.5 0.8 copy-done.8
  53.3 3.7 %all-to-all-start.1 = ((f32[8,8,8,512]{3,2,1,0:T(8,128)}), f32[8,8,8,512]{3,2,1,0:T(8,128)S(1)}, u32[]{:S(2)}, u32[]{:S(2)}) async-start(f32[8,8,8,512]{3,2,1,0:T(8,128)} %bitcast.11), calls=%async_computation.1 | async-start | bytes 2097152 | tf_op jit(solution)/shard_map/all_to_all | solution.py:326
  57.0 0.0 copy-done.13
  57.0 0.1 copy.14
  57.1 1.5 broadcast_multiply_fusion
  58.6 2.2 mul.53.w2_ref
  60.8 2.2 mul.50.w1_ref
  63.1 20.4 %all-to-all-done.1.p_ref = f32[8,8,8,512]{3,2,1,0:T(8,128)S(1)} async-done(((f32[8,8,8,512]{3,2,1,0:T(8,128)}), f32[8,8,8,512]{3,2,1,0:T(8,128)S(1)}, u32[]{:S(2)}, u32[]{:S(2)}) %all-to-all-start.1) | async-done | bytes 1048608 | tf_op jit(solution)/shard_map/all_to_all | solution.py:326
  83.5 0.0 copy-done.7
  83.5 1.0 copy-done.2
  84.6 1.0 copy-done.5
  85.6 0.8 copy-done.11
  86.4 35.5 %middle.1 = (bf16[1,8,16,128,128]{4,3,2,1,0:T(8,128)(2,1)}, f32[8,16,128,128]{3,2,1,0:T(8,128)}, f32[8,8,8,512]{3,2,1,0:T(8,128)S(1)}, f32[256,256]{1,0:T(8,128)S(1)}) custom-call(f32[8,8,8,512]{3,2,1,0:T(8,128)S(1)} %all-to-all-done.1.p_ref, bf16[1,8,16,128,128]{4,3,2,1,0:T(8,128)(2,1)} %f_ref.3, bf16[1,8,16,128,128]{4,3,2,1,0:T(8,128)(2,1)} %cot_ref.1, ...), custom_call_target="tpu_custom_call" | custom-call | tf_op jit(solution)/shard_map/middle/pallas_call | solution.py:360
  121.9 29.0 %all_to_all.21 = f32[8,8,8,512]{3,2,1,0:T(8,128)S(1)} all-to-all(f32[8,8,8,512]{3,2,1,0:T(8,128)S(1)} %get-tuple-element.14), channel_id=1, replica_groups=mesh['dp'=4,'gz'=8] {'gz'}, dimensions={0} | all-to-all | bytes 2097152 | tf_op jit(solution)/shard_map/all_to_all | solution.py:326
  150.9 9.9 %mix_adjoint.1 = (f32[512,512]{1,0:T(8,128)}, f32[2,16,32,128]{3,2,1,0:T(8,128)S(1)}) custom-call(f32[512,512]{1,0:T(8,128)S(1)} %bitcast.9, bf16[2,16,16,4096]{3,2,1,0:T(8,128)(2,1)} %r_ref.3, bf16[2,512,1024]{2,1,0:T(8,128)(2,1)S(1)} %copy-done, bf16[2,512,1024]{2,1,0:T(8,128)(2,1)S(1)} %copy-done), custom_call_target="tpu_custom_call" | custom-call | tf_op jit(solution)/shard_map/mix_adjoint/pallas_call | solution.py:375
  160.8 0.0 copy-done.12
  160.8 3.6 %all-to-all-start.3 = ((f32[8,8,8,512]{3,2,1,0:T(8,128)}), f32[8,8,8,512]{3,2,1,0:T(8,128)S(1)}, u32[]{:S(2)}, u32[]{:S(2)}) async-start(f32[8,8,8,512]{3,2,1,0:T(8,128)} %bitcast.4), calls=%async_computation.3 | async-start | bytes 2097152 | tf_op jit(solution)/shard_map/all_to_all | solution.py:326
  164.3 0.0 copy-done.9
  164.3 2.5 collective-permute-start.2
  166.8 0.5 collective-permute-start.1
  167.3 0.6 collective-permute-start
  167.9 2.4 collective-permute-start.5
  170.3 0.5 collective-permute-start.4
  170.8 9.3 %collective-permute-done.2.refs_3_ = f32[2,16,32,128]{3,2,1,0:T(8,128)S(1)} collective-permute-done((f32[2,16,32,128]{3,2,1,0:T(8,128)S(1)}, f32[2,16,32,128]{3,2,1,0:T(8,128)S(1)}, u32[]{:S(2)}, u32[]{:S(2)}) %collective-permute-start.2) | collective-permute-done | bytes 524320 | tf_op jit(solution)/shard_map/ppermute | solution.py:331
  180.1 1.5 collective-permute-start.3
  181.6 2.8 %reshape.46 = f32[16,16,16,16]{3,2,1,0:T(8,128)} reshape(f32[256,256]{1,0:T(8,128)} %copy-done.12) | data formatting | bytes 524288 | tf_op jit(solution)/shard_map/reshape | solution.py:408
  184.4 1.9 select_reduce_fusion
  186.3 61.5 %psum.7 = f32[16,16]{1,0:T(8,128)S(1)} all-reduce(f32[16,16]{1,0:T(8,128)S(1)} %select_reduce_fusion), channel_id=1, replica_groups=mesh['dp'=4,'gz'=8] {'dp','gz'}, use_global_device_ids=true, to_apply=%region_1.2 | all-reduce | flops 256 | bytes 2048 | tf_op jit(solution)/shard_map/psum | solution.py:409
  247.8 0.6 broadcast_multiply_fusion.2
  248.4 0.0 collective-permute-done.1.refs_2_
  248.4 0.0 collective-permute-done.refs_1_
  248.4 0.0 collective-permute-done.5.refs_7_
  248.4 0.0 collective-permute-done.4.refs_6_
  248.4 0.0 collective-permute-done.3.refs_5_
  248.4 9.1 %weight_gradient.1 = f32[2,16,16,4096]{3,2,1,0:T(8,128)} custom-call(f32[2,16,32,128]{3,2,1,0:T(8,128)S(1)} %copy-done.9, f32[2,16,32,128]{3,2,1,0:T(8,128)} %collective-permute-done.refs_1_, f32[2,16,32,128]{3,2,1,0:T(8,128)} %collective-permute-done.1.refs_2_, f32[2,16,32,128]{3,2,1,0:T(8,128)S(1)} %collective-permute-done.2.refs_3_, ...), custom_call_target="tpu_custom_call" | custom-call | tf_op jit(solution)/shard_map/weight_gradient/pallas_call | solution.py:398
  257.6 0.0 all-to-all-done.3.p_ref
  257.6 10.3 %input_gradient.1 = bf16[1,8,16,128,128]{4,3,2,1,0:T(8,128)(2,1)} custom-call(f32[8,8,8,512]{3,2,1,0:T(8,128)S(1)} %all-to-all-done.3.p_ref, f32[8,16,128,128]{3,2,1,0:T(8,128)} %get-tuple-element.16.part_ref, bf16[2,256,512]{2,1,0:T(8,128)(2,1)S(1)} %copy-done.3, bf16[256,256]{1,0:T(8,128)(2,1)S(1)} %copy-done.7), custom_call_target="tpu_custom_call" | custom-call | tf_op jit(solution)/shard_map/input_gradient/pallas_call | solution.py:385
  (14 shorter events, 0.0 us)
Async XLA Ops:
  0.6 42.2 %copy-start = (bf16[2,512,1024]{2,1,0:T(8,128)(2,1)S(1)}, bf16[2,512,1024]{2,1,0:T(8,128)(2,1)}, u32[]{:S(2)}) copy-start(bf16[2,512,1024]{2,1,0:T(8,128)(2,1)} %constant.19.clone.z_fwd_ref.z_inv_ref) | copy-start | bytes 6291460
  0.6 2.3 copy-start.1
  3.0 1.0 copy-start.4
  4.0 0.8 copy-start.10
  42.8 14.2 %copy-start.13 = (bf16[16,16]{1,0:T(8,128)(2,1)S(1)}, bf16[16,16]{1,0:T(8,128)(2,1)}, u32[]{:S(2)}) copy-start(bf16[16,16]{1,0:T(8,128)(2,1)} %param.13) | copy-start | bytes 1540
  51.5 1.0 copy-start.6
  52.5 0.8 copy-start.8
  53.3 30.2 %copy-start.7 = (bf16[256,256]{1,0:T(8,128)(2,1)S(1)}, bf16[256,256]{1,0:T(8,128)(2,1)}, u32[]{:S(2)}) copy-start(bf16[256,256]{1,0:T(8,128)(2,1)} %constant.18.clone.x_inv_ref) | copy-start | bytes 393220
  53.3 30.2 %all-to-all-start.1 = ((f32[8,8,8,512]{3,2,1,0:T(8,128)}), f32[8,8,8,512]{3,2,1,0:T(8,128)S(1)}, u32[]{:S(2)}, u32[]{:S(2)}) async-start(f32[8,8,8,512]{3,2,1,0:T(8,128)} %bitcast.11), calls=%async_computation.1 | async-start | bytes 2097152 | tf_op jit(solution)/shard_map/all_to_all | solution.py:326
  83.5 1.0 copy-start.2
  84.6 1.0 copy-start.5
  85.6 0.8 copy-start.11
  121.9 38.9 %copy-start.12 = (f32[256,256]{1,0:T(8,128)}, f32[256,256]{1,0:T(8,128)S(1)}, u32[]{:S(2)}) copy-start(f32[256,256]{1,0:T(8,128)S(1)} %get-tuple-element.17) | copy-start | bytes 786436
  150.9 13.4 %copy-start.9 = (f32[2,16,32,128]{3,2,1,0:T(8,128)S(1)}, f32[2,16,32,128]{3,2,1,0:T(8,128)}, u32[]{:S(2)}) copy-start(f32[2,16,32,128]{3,2,1,0:T(8,128)} %copy-done.8) | copy-start | bytes 1572868
  160.8 96.8 %all-to-all-start.3 = ((f32[8,8,8,512]{3,2,1,0:T(8,128)}), f32[8,8,8,512]{3,2,1,0:T(8,128)S(1)}, u32[]{:S(2)}, u32[]{:S(2)}) async-start(f32[8,8,8,512]{3,2,1,0:T(8,128)} %bitcast.4), calls=%async_computation.3 | async-start | bytes 2097152 | tf_op jit(solution)/shard_map/all_to_all | solution.py:326
  164.3 15.8 %collective-permute-start.2 = (f32[2,16,32,128]{3,2,1,0:T(8,128)S(1)}, f32[2,16,32,128]{3,2,1,0:T(8,128)S(1)}, u32[]{:S(2)}, u32[]{:S(2)}) collective-permute-start(f32[2,16,32,128]{3,2,1,0:T(8,128)S(1)} %copy-done.9), channel_id=1, source_target_pairs={{0,24},{8,16},{16,8},{24,0},{1,25},{9,17},{17,9},{25,1},{2,26},{10... | collective-permute-start | bytes 1572872 | tf_op jit(solution)/shard_map/ppermute | solution.py:331
  166.8 81.6 %collective-permute-start.1 = (f32[2,16,32,128]{3,2,1,0:T(8,128)S(1)}, f32[2,16,32,128]{3,2,1,0:T(8,128)}, u32[]{:S(2)}, u32[]{:S(2)}) collective-permute-start(f32[2,16,32,128]{3,2,1,0:T(8,128)S(1)} %copy-done.9), channel_id=1, source_target_pairs={{0,16},{8,24},{16,0},{24,8},{1,17},{9,25},{17,1},{25,9},{2,18},{10... | collective-permute-start | bytes 1572872 | tf_op jit(solution)/shard_map/ppermute | solution.py:331
  167.3 81.1 %collective-permute-start = (f32[2,16,32,128]{3,2,1,0:T(8,128)S(1)}, f32[2,16,32,128]{3,2,1,0:T(8,128)}, u32[]{:S(2)}, u32[]{:S(2)}) collective-permute-start(f32[2,16,32,128]{3,2,1,0:T(8,128)S(1)} %copy-done.9), channel_id=1, source_target_pairs={{0,8},{8,0},{16,24},{24,16},{1,9},{9,1},{17,25},{25,17},{2,10},{10... | collective-permute-start | bytes 1572872 | tf_op jit(solution)/shard_map/ppermute | solution.py:331
  167.9 80.5 %collective-permute-start.5 = (f32[2,16,32,128]{3,2,1,0:T(8,128)S(1)}, f32[2,16,32,128]{3,2,1,0:T(8,128)}, u32[]{:S(2)}, u32[]{:S(2)}) collective-permute-start(f32[2,16,32,128]{3,2,1,0:T(8,128)S(1)} %get-tuple-element.19.refs_4_), channel_id=1, source_target_pairs={{0,24},{8,16},{16,8},{24,0},{1,25},{9,17},{17,9},{25,1},{2,26},{10... | collective-permute-start | bytes 1572872 | tf_op jit(solution)/shard_map/ppermute | solution.py:331
  170.3 78.1 %collective-permute-start.4 = (f32[2,16,32,128]{3,2,1,0:T(8,128)S(1)}, f32[2,16,32,128]{3,2,1,0:T(8,128)}, u32[]{:S(2)}, u32[]{:S(2)}) collective-permute-start(f32[2,16,32,128]{3,2,1,0:T(8,128)S(1)} %get-tuple-element.19.refs_4_), channel_id=1, source_target_pairs={{0,16},{8,24},{16,0},{24,8},{1,17},{9,25},{17,1},{25,9},{2,18},{10... | collective-permute-start | bytes 1572872 | tf_op jit(solution)/shard_map/ppermute | solution.py:331
  180.1 68.3 %collective-permute-start.3 = (f32[2,16,32,128]{3,2,1,0:T(8,128)S(1)}, f32[2,16,32,128]{3,2,1,0:T(8,128)}, u32[]{:S(2)}, u32[]{:S(2)}) collective-permute-start(f32[2,16,32,128]{3,2,1,0:T(8,128)S(1)} %get-tuple-element.19.refs_4_), channel_id=1, source_target_pairs={{0,8},{8,0},{16,24},{24,16},{1,9},{9,1},{17,25},{25,17},{2,10},{10... | collective-permute-start | bytes 1572872 | tf_op jit(solution)/shard_map/ppermute | solution.py:331
  248.4 9.2 %copy-start.3 = (bf16[2,256,512]{2,1,0:T(8,128)(2,1)S(1)}, bf16[2,256,512]{2,1,0:T(8,128)(2,1)}, u32[]{:S(2)}) copy-start(bf16[2,256,512]{2,1,0:T(8,128)(2,1)} %constant.16.clone.y_inv_ref) | copy-start | bytes 1572868

commit v2 on v1

v2 whole, which is shorter than its diff:
```python
import functools
import math

import jax
import jax.numpy as jnp
import ml_dtypes
import numpy as np
from jax import lax
from jax.experimental import pallas as pl
from jax.experimental.pallas import tpu as pltpu
from jax.sharding import PartitionSpec as P

M = 32
QUAD = 4
CORES = 2
GROUP = 16
F32 = jnp.float32
BF16 = jnp.bfloat16
NN = (((1,), (0,)), ((), ()))
TN = (((0,), (0,)), ((), ()))
NT = (((1,), (1,)), ((), ()))
GELU_A = math.sqrt(2.0 / math.pi)
GELU_B = 0.044715


def halves(table):
    high = table.astype(np.float32).astype(ml_dtypes.bfloat16)
    low = (table - high.astype(np.float64)).astype(np.float32).astype(ml_dtypes.bfloat16)
    return high, low


def thrice(table):
    high, low = halves(table)
    return np.concatenate([high, low, high])


def trig(length, modes):
    phase = np.outer(np.arange(length), modes) % length
    angles = phase * (2.0 * math.pi / length)
    return np.cos(angles), np.sin(angles)


def complex_block(cos, sin, sign):
    return np.array([[cos, sign * sin], [-sign * sin, cos]])


def tables(width_x, width_y, depth, owned_x):
    order_y = (np.arange(M) % (M // QUAD)) * QUAD + np.arange(M) // (M // QUAD)
    cos_x, sin_x = trig(width_x, np.arange(M))
    cos_y, sin_y = trig(width_y, order_y)
    cos_z, sin_z = trig(depth, np.arange(M))
    eye4 = np.eye(QUAD)
    eye_a = np.eye(owned_x)
    y_fwd = np.einsum("pq,ryb->pyrqb", eye4, np.array([cos_y, -sin_y]))
    y_fwd = y_fwd.reshape(QUAD * width_y, 2 * QUAD * M)
    y_inv = np.einsum("pq,ryb->rpbqy", eye4, np.array([cos_y, -sin_y]))
    y_inv = y_inv.reshape(2 * QUAD * M, QUAD * width_y)
    x_fwd = np.einsum("ijxa->ajix", complex_block(cos_x, sin_x, -1.0)).reshape(2 * M, 2 * width_x)
    x_inv = np.einsum("ijxa->jxai", complex_block(cos_x, sin_x, 1.0)).reshape(2 * width_x, 2 * M)
    ones = np.ones(QUAD)
    z_fwd = np.einsum("ac,ijzk,r->zaicjrk", eye_a, complex_block(cos_z, sin_z, -1.0), ones)
    z_fwd = z_fwd.reshape(depth * owned_x * 2, owned_x * 2 * QUAD * M)
    z_inv = np.einsum("ac,ijzk,r->zcjairk", eye_a, complex_block(cos_z, sin_z, 1.0), ones)
    z_inv = z_inv.reshape(depth * owned_x * 2, owned_x * 2 * QUAD * M)
    xi_h, xi_l = halves(x_inv)
    x_inv4 = np.concatenate([xi_h, xi_l, xi_h, xi_l], axis=1)
    x_fwd2 = np.concatenate(halves(x_fwd), axis=0)
    return dict(
        y_fwd=thrice(y_fwd),
        y_inv=thrice(y_inv),
        x_fwd=x_fwd2,
        x_inv=x_inv4,
        z_fwd=np.stack(halves(z_fwd)),
        z_inv=np.stack(halves(z_inv)),
    )


def split(values):
    high = values.astype(BF16)
    return high, (values - high.astype(F32)).astype(BF16)


def dot(left, right, dims=NN):
    return lax.dot_general(left, right, dims, preferred_element_type=F32)


def x_forward(real, imag, x_fwd_ref):
    high, low = split(jnp.concatenate([real, imag], axis=0))
    both = dot(x_fwd_ref[...], high)
    rows = both.shape[0] // 2
    return both[:rows] + both[rows:] + dot(x_fwd_ref[:rows], low)


def slot(j, h, chips, first):
    c, k = j // CORES, j % CORES
    base = sum(chips + f for f in first[:h])
    if not first[h]:
        return base + c, k
    return (base + c, 0) if k == 0 else (base + chips, c)


def store_blocks(out_refs, scratch, values, me, t):
    groups, rows = scratch.shape[:2]
    for d in range(groups):
        scratch[d] = values[d * rows:(d + 1) * rows]
    for j in range(groups):
        i, lead = slot(j, 0, groups // CORES, (False,))
        out_refs[i][lead, t] = scratch[me ^ j]


def load_blocks(in_refs, scratch, flat, me, t):
    groups, rows = scratch.shape[:2]
    for j, ref in enumerate(in_refs):
        scratch[me ^ j] = ref[0, t]
    if rows % 8 == 0:
        return scratch[...].reshape(groups * rows, scratch.shape[2])
    for d in range(groups):
        flat[d * rows:(d + 1) * rows] = scratch[d]
    return flat[...]


def fields_kernel(f_ref, y_fwd_ref, x_fwd_ref, *refs):
    out_refs, v_scr = refs[:-1], refs[-1]
    channels = f_ref.shape[2]
    for t in range(f_ref.shape[1]):
        real, imag = [], []
        for j in range(channels // QUAD):
            planes = [f_ref[0, t, QUAD * j + p] for p in range(QUAD)]
            g = dot(jnp.concatenate(planes + planes, axis=1), y_fwd_ref[:2 * QUAD * f_ref.shape[4]])
            half = g.shape[1] // 2
            real.append(g[:, :half])
            imag.append(g[:, half:])
        values = x_forward(jnp.concatenate(real, axis=1), jnp.concatenate(imag, axis=1), x_fwd_ref)
        store_blocks(out_refs, v_scr.at[t], values, lax.axis_index("gz"), t)


def inverse_planes(p, x_inv_ref, y_inv_ref):
    high, low = split(p)
    q = dot(x_inv_ref[...], jnp.concatenate([high, high, low, low], axis=0))
    q_high, q_low = split(q)
    rows = q.shape[0] // 2
    wide = QUAD * M
    for j in range(q.shape[1] // wide):
        here = slice(j * wide, (j + 1) * wide)
        high = [q_high[:rows, here], q_high[rows:, here]]
        low = [q_low[:rows, here], q_low[rows:, here]]
        yield j, dot(jnp.concatenate(high + high + low, axis=1), y_inv_ref[...])


def middle_kernel(groups, *refs):
    in_refs, inputs, (act_ref, part_ref, pg_ref), out_refs, scratch = cut(
        refs, groups, 8, 3, groups // CORES, 8)
    f_ref, cot_ref, w_ref, spread_ref, y_fwd_ref, x_fwd_ref, y_inv_ref, x_inv_ref = inputs
    p_scr, flat, spec, g_high, g_low, w1_ref, w2_ref, pg_scr = scratch
    me = lax.axis_index("gz")
    channels, width_x, width_y = f_ref.shape[2:]
    group = GROUP
    side = channels * group
    same = (lax.broadcasted_iota(jnp.int32, (side, side), 0) % group
            == lax.broadcasted_iota(jnp.int32, (side, side), 1) % group)

    @pl.when(pl.program_id(0) == 0)
    def _():
        pg_scr[...] = jnp.zeros_like(pg_scr)
        spread = spread_ref[...]
        for ref, dims in ((w1_ref, NT), (w2_ref, NN)):
            rows = dot(spread, w_ref[...], dims).astype(BF16)
            ref[...] = jnp.where(same, dot(rows, spread, NT), 0.0).astype(BF16)

    for t in range(f_ref.shape[1]):
        for j, value in inverse_planes(load_blocks(in_refs, p_scr.at[t], flat.at[t], me, t), x_inv_ref, y_inv_ref):
            for p in range(QUAD):
                spec[t, QUAD * j + p] = value[:, p * width_y:(p + 1) * width_y]

        rows = channels * group

        def step(u, carry):
            first = pl.multiple_of(u * 2 * group, 2 * group)
            cells = [pl.ds(first, group), pl.ds(first + group, group)]

            def both(read):
                return jnp.concatenate([read(s).reshape(rows, width_y) for s in cells], axis=1)

            f = both(lambda s: f_ref[0, t, :, s, :])
            pre = dot(w1_ref[...], f) + both(lambda s: spec[t, :, s, :])
            square = pre * pre
            t_val = jnp.tanh(GELU_A * pre * (1.0 + GELU_B * square))
            cdf = 0.5 + 0.5 * t_val
            act = (pre * cdf).astype(BF16)
            slope = cdf + pre * (0.5 - 0.5 * t_val * t_val) * (GELU_A + 3.0 * GELU_A * GELU_B * square)
            g = both(lambda s: cot_ref[0, t, :, s, :]).astype(F32) * slope
            high, low = split(g)
            part = dot(w2_ref[...], high) + dot(w2_ref[...], low)
            pg = None
            for i, s in enumerate(cells):
                lanes = slice(i * width_y, (i + 1) * width_y)
                shape = (channels, group, width_y)
                act_ref[0, t, :, s, :] = act[:, lanes].reshape(shape)
                part_ref[t, :, s, :] = part[:, lanes].reshape(shape)
                g_high[t, :, s, :] = high[:, lanes].reshape(shape)
                g_low[t, :, s, :] = low[:, lanes].reshape(shape)
            pg_scr[...] += dot(f, high, NT) + dot(f, low, NT)
            return carry

        lax.fori_loop(0, width_x // (2 * group), step, 0, unroll=True)

        real, imag = [], []
        for j in range(channels // QUAD):
            high, low = [[r[t, QUAD * j + p] for p in range(QUAD)] for r in (g_high, g_low)]
            v = dot(jnp.concatenate(high + high + low, axis=1), y_fwd_ref[...])
            half = v.shape[1] // 2
            real.append(v[:, :half])
            imag.append(v[:, half:])
        values = x_forward(jnp.concatenate(real, axis=1), jnp.concatenate(imag, axis=1), x_fwd_ref)
        store_blocks(out_refs, p_scr.at[t], values, me, t)

    @pl.when(pl.program_id(0) == pl.num_programs(0) - 1)
    def _():
        spread = spread_ref[...].astype(F32)
        kept = jnp.where(same, pg_scr[...], 0.0)
        right = lax.dot_general(kept, spread, NN, precision=lax.Precision.HIGHEST, preferred_element_type=F32)
        pg_ref[...] = lax.dot_general(spread, right, TN, precision=lax.Precision.HIGHEST, preferred_element_type=F32)


def final_kernel(groups, *refs):
    in_refs, (part_ref, y_inv_ref, x_inv_ref, out_ref, p_scr, flat) = cut(refs, groups, 6)
    me = lax.axis_index("gz")
    width_y = out_ref.shape[4]
    for t in range(out_ref.shape[1]):
        for j, value in inverse_planes(load_blocks(in_refs, p_scr.at[t], flat.at[t], me, t), x_inv_ref, y_inv_ref):
            for p in range(QUAD):
                c = QUAD * j + p
                out_ref[0, t, c] = (value[:, p * width_y:(p + 1) * width_y] + part_ref[t, c]).astype(BF16)


def lane_quad(shape):
    return lax.broadcasted_iota(jnp.int32, shape, len(shape) - 1) // M


def depth_forward(in_refs, s_scr, z_fwd_ref, spec_ref, scale):
    me = lax.axis_index("gz")
    groups = s_scr.shape[0]
    tall = s_scr.shape[1] * groups // len(in_refs)
    for i, ref in enumerate(in_refs):
        h, j = i // groups, i % groups
        s_scr[me ^ j, h * tall:(h + 1) * tall] = ref[0]
    high, low = split(s_scr[...].reshape(-1, s_scr.shape[2]))
    v = dot(high, z_fwd_ref[0], TN) + dot(high, z_fwd_ref[1], TN) + dot(low, z_fwd_ref[0], TN)
    tall = M // QUAD
    wide = QUAD * M
    channels = v.shape[0] // M
    v = v.reshape(channels, QUAD, tall, v.shape[1])
    quad = lane_quad((channels, tall, wide))
    for a in range(v.shape[3] // (2 * wide)):
        for part in range(2):
            lanes = slice((2 * a + part) * wide, (2 * a + part + 1) * wide)
            u = v[:, 0, :, lanes]
            for r in range(1, QUAD):
                u = jnp.where(quad == r, v[:, r, :, lanes], u)
            spec_ref[part, :channels, a * tall:(a + 1) * tall, :] = u * scale if scale != 1.0 else u


def depth_inverse(spec_ref, z_inv_ref, s_scr, out_refs, first):
    channels, places, wide = spec_ref.shape[1:]
    tall = M // QUAD
    quad = lane_quad((channels, tall, wide))
    pieces = []
    for a in range(places // tall):
        for part in range(2):
            v = spec_ref[part, :, a * tall:(a + 1) * tall, :]
            masked = jnp.stack([jnp.where(quad == r, v, 0.0) for r in range(QUAD)], axis=1)
            pieces.append(masked.reshape(channels * M, wide))
    high, low = split(jnp.concatenate(pieces, axis=1))
    values = dot(z_inv_ref[0], high, NT) + dot(z_inv_ref[1], high, NT) + dot(z_inv_ref[0], low, NT)
    s_scr[...] = values.reshape(s_scr.shape)
    me = lax.axis_index("gz")
    groups = s_scr.shape[0]
    tall = s_scr.shape[1] // len(first)
    for h in range(len(first)):
        for j in range(groups):
            i, lead = slot(j, h, groups // CORES, first)
            out_refs[i][lead] = s_scr[me ^ j, h * tall:(h + 1) * tall]


def cut(refs, *counts):
    pieces = []
    for n in counts:
        pieces.append(refs[:n])
        refs = refs[n:]
    return pieces


def mix_kernel(count_in, count_out, first, scale, *refs):
    in_refs, (r_ref, z_fwd_ref, z_inv_ref, u_ref), out_refs, (v_scr, s_scr) = cut(refs, count_in, 4, count_out, 2)
    channels, places, wide = u_ref.shape[1:]
    depth_forward(in_refs, s_scr, z_fwd_ref, u_ref, 1.0)

    def step(q, carry):
        lanes = pl.ds(pl.multiple_of(q * wide, wide), wide)
        real = jnp.zeros((channels, wide), F32)
        imag = jnp.zeros((channels, wide), F32)
        for c in range(channels):
            w_re = r_ref[0, c, :, lanes].astype(F32)
            w_im = r_ref[1, c, :, lanes].astype(F32)
            u_re = u_ref[0, c, pl.ds(q, 1), :]
            u_im = u_ref[1, c, pl.ds(q, 1), :]
            real += u_re * w_re - u_im * w_im
            imag += u_re * w_im + u_im * w_re
        v_scr[0, :, pl.ds(q, 1), :] = (real * scale)[:, None, :]
        v_scr[1, :, pl.ds(q, 1), :] = (imag * scale)[:, None, :]
        return carry

    lax.fori_loop(0, places, step, 0)
    depth_inverse(v_scr, z_inv_ref, s_scr, out_refs, first)


def adjoint_kernel(count_in, count_out, first, scale, *refs):
    in_refs, (point_ref, r_ref, z_fwd_ref, z_inv_ref, dv_ref), out_refs, (du_scr, s_scr) = cut(
        refs, count_in, 5, count_out, 2)
    channels, places, wide = du_scr.shape[1:]
    dv_ref[:, channels:] = jnp.zeros((2, 1, places, wide), F32)
    dv_ref[0, channels, 0:point_ref.shape[0]] = point_ref[...]
    depth_forward(in_refs, s_scr, z_fwd_ref, dv_ref, scale)

    def step(q, carry):
        lanes = pl.ds(pl.multiple_of(q * wide, wide), wide)
        d_re = dv_ref[0, :channels, pl.ds(q, 1), :].reshape(channels, wide)
        d_im = dv_ref[1, :channels, pl.ds(q, 1), :].reshape(channels, wide)
        for c in range(channels):
            w_re = r_ref[0, c, :, lanes].astype(F32)
            w_im = r_ref[1, c, :, lanes].astype(F32)
            du_scr[0, c, pl.ds(q, 1), :] = jnp.sum(d_re * w_re + d_im * w_im, axis=0, keepdims=True)
            du_scr[1, c, pl.ds(q, 1), :] = jnp.sum(d_im * w_re - d_re * w_im, axis=0, keepdims=True)
        return carry

    lax.fori_loop(0, places, step, 0)
    depth_inverse(du_scr, z_inv_ref, s_scr, out_refs, first)


def weight_grad_kernel(scale, *refs):
    u_ref, dv_refs, out_ref = refs[0], refs[1:-1], refs[-1]
    count = len(dv_refs)
    me = lax.axis_index("dp")
    channels, places, wide = u_ref.shape[2:]
    for q in range(places):
        lanes = slice(q * wide, (q + 1) * wide)
        dv = [[r[part, :channels, q, :] * scale for part in range(2)] for r in dv_refs]
        for c in range(channels):
            real = imag = None
            for s in range(count):
                u_re = u_ref[me ^ s, 0, c, q:q + 1, :]
                u_im = u_ref[me ^ s, 1, c, q:q + 1, :]
                d_re, d_im = dv[s]
                t_re = u_re * d_re + u_im * d_im
                t_im = u_re * d_im - u_im * d_re
                real = t_re if real is None else real + t_re
                imag = t_im if imag is None else imag + t_im
            out_ref[0, c, :, lanes] = real
            out_ref[1, c, :, lanes] = imag


def params(steps, megabytes=60):
    return pltpu.CompilerParams(
        dimension_semantics=("arbitrary",) * steps, vmem_limit_bytes=megabytes * 1024 * 1024
    )


def cost(micros):
    return pl.CostEstimate(flops=int(micros * 1.1e9), bytes_accessed=int(micros * 3.5e6), transcendentals=0)


def whole_spec(array):
    rank = len(array.shape)
    return pl.BlockSpec(tuple(array.shape), lambda *i: (0,) * rank)


def shards(fields, cotangent, spectral_weight, pointwise_weight):
    groups = lax.axis_size("gz")
    samples = lax.axis_size("dp")
    _, near, channels, width_x, width_y = fields.shape
    depth = near * groups
    owned = M // groups
    rows = 2 * owned
    wide = channels * M
    places = spectral_weight.shape[3] // (QUAD * M)
    total_modes = M * M * M
    cells = samples * width_x * width_y * depth
    scale = 1.0 / math.sqrt(width_x * width_y * depth * total_modes)
    tab = {k: jnp.asarray(v) for k, v in tables(width_x, width_y, depth, owned).items()}

    chips = groups // CORES
    cut_out = 2
    part_near = near // cut_out
    batch = 2
    plane_shape = (1, batch, channels, width_x, width_y)
    plane = pl.BlockSpec(plane_shape, lambda z: (0, z, 0, 0, 0))

    def block(planes):
        return pl.BlockSpec((CORES, planes, rows, wide), lambda z: (0, z, 0, 0))

    def scratch(planes):
        return [pltpu.VMEM((planes, groups, rows, wide), F32),
                pltpu.VMEM((planes, groups * rows if rows % 8 else 8, wide), F32)]

    spec_shape = jax.ShapeDtypeStruct((2, channels, places, QUAD * M), F32)

    def sent(planes):
        return [jax.ShapeDtypeStruct((CORES, planes, rows, wide), F32)] * chips

    def hop(values, j):
        return lax.ppermute(values, "gz", [(i, i ^ j) for i in range(groups)])

    far_first = sorted(range(1, chips), key=lambda c: (-(c & (chips // 2)), c))

    def cross(blocks):
        got = [blocks[0]] + [None] * (chips - 1)
        for c in far_first:
            got[c] = hop(blocks[c], CORES * c)
        return got

    def swap(got):
        swapped = hop(jnp.stack([g[1] for g in got]), 1)
        return [(got[j // CORES], 0) if j % CORES == 0 else (swapped, j // CORES) for j in range(groups)]

    def swap_last(blocks):
        return swap(cross(blocks))

    def swap_first(blocks):
        *near_blocks, crossing = blocks
        swapped = hop(crossing, 1)
        got = [None] * chips
        for c in far_first:
            got[c] = hop(jnp.concatenate([near_blocks[c], swapped[c:c + 1]]), CORES * c)
        return [(near_blocks[0], 0), (swapped, 0)] + [(got[j // CORES], j % CORES) for j in range(CORES, groups)]

    def reshaped(arrays, *shape):
        return [v.reshape(v.shape[0], *shape) for v in arrays]

    def gather(values):
        pieces = [values]
        for k in range(1, samples):
            pieces.append(lax.ppermute(values, "dp", [(i, i ^ k) for i in range(samples)]))
        return pieces

    def plane_specs(arrived, planes):
        def one(lead):
            return pl.BlockSpec((1, planes, rows, wide), lambda z: (lead, z, 0, 0))
        return [v for v, _ in arrived], [one(lead) for _, lead in arrived]

    def mix_call(kernel, name, arrived, first, factor, *extra):
        pieces = [p for half in arrived for p in half]
        tall = near // len(arrived) * rows
        operands = [v.reshape(v.shape[0], tall, wide) for v, _ in pieces]

        def one(lead):
            return pl.BlockSpec((1, tall, wide), lambda i: (lead, 0, 0))

        constants = [*extra, spectral_weight, tab["z_fwd"], tab["z_inv"]]
        made = jax.ShapeDtypeStruct((2, channels + len(extra), places, QUAD * M), F32)
        halves = len(first)
        low = near // halves * rows
        outs = []
        for f in first:
            outs += [jax.ShapeDtypeStruct((1 if f else CORES, low, wide), F32)] * chips
            outs += [jax.ShapeDtypeStruct((chips, low, wide), F32)] * f
        result = pl.pallas_call(
            functools.partial(kernel, len(operands), len(outs), first, factor),
            grid=(1,),
            in_specs=[one(lead) for _, lead in pieces] + [whole_spec(v) for v in constants],
            out_specs=[whole_spec(made)] + [whole_spec(v) for v in outs],
            out_shape=[made] + outs,
            scratch_shapes=[pltpu.VMEM(spec_shape.shape, F32), pltpu.VMEM((groups, near * rows, wide), F32)],
            compiler_params=params(1),
            name=name,
            cost_estimate=cost(9),
        )(*operands, *constants)
        blocks = reshaped(result[1:], near // halves, rows, wide)
        return result[0], cut(blocks, *[chips + f for f in first])

    forward = pl.pallas_call(
        fields_kernel,
        grid=(near // batch,),
        in_specs=[plane, whole_spec(tab["y_fwd"]), whole_spec(tab["x_fwd"])],
        out_specs=[block(batch)] * chips,
        out_shape=sent(near),
        scratch_shapes=scratch(batch)[:1],
        compiler_params=params(1),
        name="fields_forward",
        cost_estimate=cost(5),
    )(fields, tab["y_fwd"], tab["x_fwd"])
    arrived = [swap_last(forward)]

    u_spec, mixed = mix_call(mix_kernel, "mix_modes", arrived, (False, True), scale)
    planes = [swap_last(mixed[0]), swap_first(mixed[1])]
    u_all = lax.all_gather(u_spec, "dp")

    side = channels * GROUP
    spread = jnp.asarray(np.kron(np.eye(channels), np.ones((GROUP, 1))).astype(ml_dtypes.bfloat16))
    scratch_planes = (channels, width_x, width_y)

    def middle(h, arrived, act):
        first = h * part_near
        here = pl.BlockSpec((1, 1) + plane_shape[2:], lambda z: (0, first + z, 0, 0, 0))
        constants = [pointwise_weight, spread, tab["y_fwd"], tab["x_fwd"], tab["y_inv"], tab["x_inv"]]
        operands, in_specs = plane_specs(arrived, 1)
        operands = [*operands, fields, cotangent, *constants]
        in_specs = in_specs + [here, here] + [whole_spec(v) for v in constants]
        body = functools.partial(middle_kernel, groups)
        aliases = {}
        if act is not None:
            aliases = {len(operands): 0, len(operands) + 1: 1}
            operands += act
            in_specs += [pl.BlockSpec(memory_space=pl.ANY)] * 2
            plain = body

            def body(*refs):
                n = len(in_specs)
                plain(*refs[:n - 2], *refs[n:])

        return pl.pallas_call(
            body,
            grid=(part_near,),
            in_specs=in_specs,
            out_specs=[here, pl.BlockSpec((1,) + scratch_planes, lambda z: (first + z, 0, 0, 0)),
                       pl.BlockSpec((channels, channels), lambda z: (0, 0))] + [block(1)] * chips,
            out_shape=[jax.ShapeDtypeStruct(fields.shape, BF16),
                       jax.ShapeDtypeStruct((near, *scratch_planes), F32),
                       jax.ShapeDtypeStruct((channels, channels), F32)] + sent(part_near),
            scratch_shapes=[*scratch(1), pltpu.VMEM((1, *scratch_planes), F32),
                            pltpu.VMEM((1, *scratch_planes), BF16),
                            pltpu.VMEM((1, *scratch_planes), BF16),
                            pltpu.VMEM((side, side), BF16), pltpu.VMEM((side, side), BF16),
                            pltpu.VMEM((side, side), F32)],
            input_output_aliases=aliases,
            compiler_params=params(1),
            name="middle%d" % h,
            cost_estimate=cost(18),
        )(*operands)

    act, points, arrived = None, [], []
    for h in range(cut_out):
        if h:
            point, values = lax.optimization_barrier((points[-1], [v for v, _ in planes[h]]))
            points[-1] = point
            planes[h] = [(v, lead) for v, (_, lead) in zip(values, planes[h])]
        layer_output, part, point, *blocks = middle(h, planes[h], act)
        act = [layer_output, part]
        points.append(point)
        if h:
            blocks, crossed = lax.optimization_barrier((blocks, crossed))
        else:
            crossed = cross(blocks)
        if h:
            arrived = [swap(crossed)]
            crossed = cross(blocks)
            point = sum(points).reshape(-1, QUAD * M)
            k = 1
            while k < groups:
                point = point + hop(point, k)
                k *= 2
            crossed[0], point = lax.optimization_barrier((crossed[0], point))
            arrived.append(swap(crossed))

    last = arrived[-1][1][0]
    last, u_all = lax.optimization_barrier((last, u_all))
    arrived[-1] = [(last if j % CORES else v, lead) for j, (v, lead) in enumerate(arrived[-1])]

    dv_spec, adjoint = mix_call(adjoint_kernel, "mix_adjoint", arrived, (False,), scale, point)
    crossed = cross(adjoint[0])
    dv_all = gather(dv_spec)
    planes = swap(crossed)
    operands, in_specs = plane_specs(planes, batch)
    point = sum(v[0, channels, :point.shape[0]] for v in dv_all).reshape(channels, channels)
    pointwise_grad = point * (1.0 / math.sqrt(cells))

    input_grad = pl.pallas_call(
        functools.partial(final_kernel, groups),
        grid=(near // batch,),
        in_specs=in_specs + [pl.BlockSpec((batch,) + scratch_planes, lambda z: (z, 0, 0, 0)),
                             whole_spec(tab["y_inv"]), whole_spec(tab["x_inv"])],
        out_specs=plane,
        out_shape=jax.ShapeDtypeStruct(fields.shape, BF16),
        scratch_shapes=scratch(batch),
        compiler_params=params(1),
        name="input_gradient",
        cost_estimate=cost(10),
    )(*operands, part, tab["y_inv"], tab["x_inv"])

    tall = 8
    spec_block = pl.BlockSpec((2, channels + 1, tall, QUAD * M), lambda q: (0, 0, q, 0))
    spectral_grad = pl.pallas_call(
        functools.partial(weight_grad_kernel, math.sqrt(total_modes / cells)),
        grid=(places // tall,),
        in_specs=[pl.BlockSpec((samples, 2, channels, tall, QUAD * M), lambda q: (0, 0, 0, q, 0))]
        + [spec_block] * samples,
        out_specs=pl.BlockSpec((2, channels, channels, tall * QUAD * M), lambda q: (0, 0, 0, q)),
        out_shape=jax.ShapeDtypeStruct(spectral_weight.shape, F32),
        compiler_params=params(1),
        name="weight_gradient",
        cost_estimate=cost(9),
    )(u_all, *dv_all)

    return layer_output, input_grad, pointwise_grad, spectral_grad


def solution(mesh):
    placed = (
        P("dp", "gz", None, None, None),
        P("dp", "gz", None, None, None),
        P(None, None, None, "gz"),
        P(),
    )
    return jax.shard_map(
        shards,
        mesh=mesh,
        in_specs=placed,
        out_specs=(
            P("dp", "gz", None, None, None),
            P("dp", "gz", None, None, None),
            P(),
            P(None, None, None, "gz"),
        ),
        check_vma=False,
    )
```

time: 269 us -> 205 us (0.76)
  blocking collectives: 123 us -> 0 us
  waiting for transfers between devices: 29.7 us -> 57.2 us
  starting transfers between devices: 15.2 us -> 39.1 us
  between operations: 0.77 us -> 14.6 us
  local copies, waits for them, and re-layouts: 16.3 us -> 7.38 us
  Pallas kernels: 78.7 us -> 81.6 us
    all_to_all x2 -> x0, blocking collectives: 61.7 us -> none  [exchange(): return lax.all_to_all(values, 'gz', 0, 0, tiled=True)]
    psum x1 -> x0, blocking collectives: 61.5 us -> none  [shards(): pointwise_grad = lax.psum(point, ('dp', 'gz')) * (1.0 / math.sqrt(cells))]
    ppermute x0 -> x27, waiting for transfers between devices: none -> 54.5 us  [hop(): return lax.ppermute(values, 'gz', [(i, i ^ j) for i in range(groups)])]
    ppermute x0 -> x27, starting transfers between devices: none -> 35.5 us  [hop(): return lax.ppermute(values, 'gz', [(i, i ^ j) for i in range(groups)])]
    all_to_all x2 -> x0, waiting for transfers between devices: 20.4 us -> none  [exchange(): return lax.all_to_all(values, 'gz', 0, 0, tiled=True)]
    all_to_all x2 -> x0, starting transfers between devices: 7.25 us -> none  [exchange(): return lax.all_to_all(values, 'gz', 0, 0, tiled=True)]
    ppermute x6 -> x3, waiting for transfers between devices: 9.27 us -> 2.72 us  [gather(): lax.ppermute(values, 'dp', [(i, i ^ k) for i in range(samples)])]
    unnamed x28 -> x58, local copies, waits for them, and re-layouts: 8.93 us -> 2.97 us
  transfers between devices with their start and end apart: 8 -> 31, of which waited for: 2 -> 13; matrix products, arithmetic and copies ran while one was open for 4% -> 4% of each run, Pallas kernels for 3% -> 21%
where the time goes in v2:
time: 205 us
  Pallas kernels  81.6 us (40%)
  waiting for transfers between devices  57.2 us (28%)
  starting transfers between devices  39.1 us (19%)
  between operations  14.6 us (7%)
  local copies, waits for them, and re-layouts  7.38 us (4%)
  other arithmetic  4.75 us (2%)
    ppermute x27, waiting for transfers between devices, hop(): return lax.ppermute(values, 'gz', [(i, i ^ j) for i in range(groups)])  54.5 us
    ppermute x27, starting transfers between devices, hop(): return lax.ppermute(values, 'gz', [(i, i ^ j) for i in range(groups)])  35.5 us
    pallas_call x2, Pallas kernels, middle(): pl.pallas_call(body, grid=(part_near,), in_specs=in_specs, out_specs=[her...  33 us
    pallas_call x2, Pallas kernels, mix_call(): pl.pallas_call(functools.partial(kernel, len(operands), len(outs), first,...  23.1 us
    pallas_call x1, Pallas kernels, shards(): pl.pallas_call(functools.partial(final_kernel, groups), grid=(near // bat...  9.32 us
    pallas_call x1, Pallas kernels, shards(): pl.pallas_call(functools.partial(weight_grad_kernel, math.sqrt(total_mode...  9.28 us
    pallas_call x1, Pallas kernels, shards(): pl.pallas_call(fields_kernel, grid=(near // batch,), in_specs=[plane, who...  6.95 us
  transfers between devices with their start and end apart: 31, of which 13 were waited for; matrix products, arithmetic and copies ran while one was open for 4% of the time, Pallas kernels for 21%

profile of v2, /device:TPU:0, one launch (start us, length us, event | category | flops | bytes accessed | tf_op | source)
XLA Modules:
  0.0 204.6 jit_solution(15553130220093721016)
XLA Ops:
  7.2 6.9 %fields_forward.1 = (f32[2,8,8,512]{3,2,1,0:T(8,128)}, f32[2,8,8,512]{3,2,1,0:T(8,128)}, f32[2,8,8,512]{3,2,1,0:T(8,128)}, f32[2,8,8,512]{3,2,1,0:T(8,128)}) custom-call(bf16[1,8,16,128,128]{4,3,2,1,0:T(8,128)(2,1)} %refs_8_.5, bf16[1536,256]{1,0:T(8,128)(2,1)} %constant.14.clone.y_fwd_ref.refs_12_, bf16[128,256]{1,0:T(8,128)(2,1)} %constant.16.clone.x_fwd_ref.refs_13_), custom_call_target="tpu_custom_call" | custom-call | flops 5500000256 | bytes 17500000 | tf_op jit(solution)/shard_map/fields_forward/pallas_call | solution.py:480
  14.2 3.0 %collective-permute-start = (f32[2,8,8,512]{3,2,1,0:T(8,128)}, f32[2,8,8,512]{3,2,1,0:T(8,128)S(1)}, u32[]{:S(2)}, u32[]{:S(2)}) collective-permute-start(f32[2,8,8,512]{3,2,1,0:T(8,128)} %get-tuple-element.59), channel_id=1, source_target_pairs={{0,2},{1,3},{2,0},{3,1},{4,6},{5,7},{6,4},{7,5},{8,10},{9,11},{10,... | collective-permute-start | bytes 786440 | tf_op jit(solution)/shard_map/ppermute | solution.py:411
  17.2 2.6 %collective-permute-start.1 = (f32[2,8,8,512]{3,2,1,0:T(8,128)}, f32[2,8,8,512]{3,2,1,0:T(8,128)S(1)}, u32[]{:S(2)}, u32[]{:S(2)}) collective-permute-start(f32[2,8,8,512]{3,2,1,0:T(8,128)} %get-tuple-element.60), channel_id=1, source_target_pairs={{0,4},{1,5},{2,6},{3,7},{4,0},{5,1},{6,2},{7,3},{8,12},{9,13},{10,... | collective-permute-start | bytes 786440 | tf_op jit(solution)/shard_map/ppermute | solution.py:411
  19.8 0.9 slice.87
  20.7 7.9 %collective-permute-done = f32[2,8,8,512]{3,2,1,0:T(8,128)S(1)} collective-permute-done((f32[2,8,8,512]{3,2,1,0:T(8,128)}, f32[2,8,8,512]{3,2,1,0:T(8,128)S(1)}, u32[]{:S(2)}, u32[]{:S(2)}) %collective-permute-start) | collective-permute-done | bytes 262176 | tf_op jit(solution)/shard_map/ppermute | solution.py:411
  28.6 10.2 %collective-permute-done.1 = f32[2,8,8,512]{3,2,1,0:T(8,128)S(1)} collective-permute-done((f32[2,8,8,512]{3,2,1,0:T(8,128)}, f32[2,8,8,512]{3,2,1,0:T(8,128)S(1)}, u32[]{:S(2)}, u32[]{:S(2)}) %collective-permute-start.1) | collective-permute-done | bytes 262176 | tf_op jit(solution)/shard_map/ppermute | solution.py:411
  39.0 1.9 collective-permute-done.3
  40.9 0.8 copy-done.22
  41.6 11.5 %mix_modes.1 = (f32[2,16,32,128]{3,2,1,0:T(8,128)}, f32[2,32,512]{2,1,0:T(8,128)}, f32[2,32,512]{2,1,0:T(8,128)}, f32[2,32,512]{2,1,0:T(8,128)}, f32[2,32,512]{2...) custom-call(f32[2,64,512]{2,1,0:T(8,128)} %bitcast.34, ...), custom_call_target="tpu_custom_call" | custom-call | flops 9900000256 | bytes 31500000 | tf_op jit(solution)/shard_map/mix_modes/pallas_call | solution.py:466
  53.1 4.7 %collective-permute-start.4 = (f32[2,4,8,512]{3,2,1,0:T(8,128)}, f32[2,4,8,512]{3,2,1,0:T(8,128)S(1)}, u32[]{:S(2)}, u32[]{:S(2)}) collective-permute-start(f32[2,4,8,512]{3,2,1,0:T(8,128)} %bitcast.69), channel_id=1, source_target_pairs={{0,2},{1,3},{2,0},{3,1},{4,6},{5,7},{6,4},{7,5},{8,10},{9,11},{10,... | collective-permute-start | bytes 393224 | tf_op jit(solution)/shard_map/ppermute | solution.py:411
  57.9 1.1 collective-permute-start.5
  58.9 1.4 collective-permute-start.6
  60.4 0.8 slice_bitcast_fusion.1
  61.2 2.5 %collective-permute-done.4.refs_2_ = f32[2,4,8,512]{3,2,1,0:T(8,128)S(1)} collective-permute-done((f32[2,4,8,512]{3,2,1,0:T(8,128)}, f32[2,4,8,512]{3,2,1,0:T(8,128)S(1)}, u32[]{:S(2)}, u32[]{:S(2)}) %collective-permute-start.4) | collective-permute-done | bytes 131104 | tf_op jit(solution)/shard_map/ppermute | solution.py:411
  63.8 7.2 %collective-permute-done.5.refs_4_ = f32[2,4,8,512]{3,2,1,0:T(8,128)S(1)} collective-permute-done((f32[2,4,8,512]{3,2,1,0:T(8,128)}, f32[2,4,8,512]{3,2,1,0:T(8,128)S(1)}, u32[]{:S(2)}, u32[]{:S(2)}) %collective-permute-start.5) | collective-permute-done | bytes 131104 | tf_op jit(solution)/shard_map/ppermute | solution.py:411
  71.2 0.9 pad_maximum_fusion.6
  72.1 3.3 %collective-permute-start.10 = (f32[2,4,8,512]{3,2,1,0:T(8,128)S(1)}, f32[2,4,8,512]{3,2,1,0:T(8,128)S(1)}, u32[]{:S(2)}, u32[]{:S(2)}) collective-permute-start(f32[2,4,8,512]{3,2,1,0:T(8,128)S(1)} %pad_maximum_fusion.6), channel_id=1, source_target_pairs={{0,4},{1,5},{2,6},{3,7},{4,0},{5,1},{6,2},{7,3},{8,12},{9,13},{10,... | collective-permute-start | bytes 393224 | tf_op jit(solution)/shard_map/ppermute | solution.py:411
  75.4 0.8 pad_maximum_fusion.7
  76.2 1.5 collective-permute-start.11
  77.7 0.8 pad_maximum_fusion.5
  79.3 16.3 %middle0.1 = (bf16[1,8,16,128,128]{4,3,2,1,0:T(8,128)(2,1)}, f32[8,16,128,128]{3,2,1,0:T(8,128)}, f32[16,16]{1,0:T(8,128)}, f32[2,4,8,512]{3,2,1,0:T(8,128)}, f3...) custom-call(f32[2,4,8,512]{3,2,1,0:T(8,128)} %bitcast.48, f32[4,4,8,512]{3,2,1,0:T(8,128)} %copy-done.23, ...), custom_call_target="tpu_custom_call" | custom-call | flops 19800000512 | bytes 63000000 | tf_op jit(solution)/shard_map/middle0/pallas_call | solution.py:520
  95.8 2.1 %collective-permute-start.12 = (f32[2,4,8,512]{3,2,1,0:T(8,128)}, f32[2,4,8,512]{3,2,1,0:T(8,128)S(1)}, u32[]{:S(2)}, u32[]{:S(2)}) collective-permute-start(f32[2,4,8,512]{3,2,1,0:T(8,128)} %get-tuple-element.88), channel_id=1, source_target_pairs={{0,2},{1,3},{2,0},{3,1},{4,6},{5,7},{6,4},{7,5},{8,10},{9,11},{10,... | collective-permute-start | bytes 393224 | tf_op jit(solution)/shard_map/ppermute | solution.py:411
  97.9 1.0 collective-permute-start.13
  98.9 1.4 collective-permute-start.14
  100.3 16.6 %middle1.1 = (bf16[1,8,16,128,128]{4,3,2,1,0:T(8,128)(2,1)}, f32[8,16,128,128]{3,2,1,0:T(8,128)}, f32[16,16]{1,0:T(8,128)}, f32[2,4,8,512]{3,2,1,0:T(8,128)}, f3...) custom-call(f32[1,4,8,512]{3,2,1,0:T(8,128)} %bitcast.70, ...), custom_call_target="tpu_custom_call", output_to_operand_aliasing={{0}: (16, {}), {1}: (17, {})} | custom-call | flops 19800000512 | bytes 63000000 | tf_op jit(solution)/shard_map/middle1/pallas_call | solution.py:520
  117.0 1.1 collective-permute-start.19
  118.2 1.9 collective-permute-start.20
  120.1 1.4 collective-permute-start.21
  122.3 1.1 collective-permute-done.16
  123.6 3.4 %collective-permute-done.17 = f32[2,128]{1,0:T(2,128)S(1)} collective-permute-done((f32[2,128]{1,0:T(2,128)S(1)}, f32[2,128]{1,0:T(2,128)S(1)}, u32[]{:S(2)}, u32[]{:S(2)}) %collective-permute-start.17) | collective-permute-done | bytes 1056 | tf_op jit(solution)/shard_map/ppermute | solution.py:411
  127.0 2.2 %collective-permute-start.18 = (f32[2,128]{1,0:T(2,128)S(1)}, f32[2,128]{1,0:T(2,128)S(1)}, u32[]{:S(2)}, u32[]{:S(2)}) collective-permute-start(f32[2,128]{1,0:T(2,128)S(1)} %add.29), channel_id=1, source_target_pairs={{0,4},{1,5},{2,6},{3,7},{4,0},{5,1},{6,2},{7,3},{8,12},{9,13},{10,... | collective-permute-start | bytes 3080 | tf_op jit(solution)/shard_map/ppermute | solution.py:411
  129.2 2.4 %collective-permute-done.18 = f32[2,128]{1,0:T(2,128)S(1)} collective-permute-done((f32[2,128]{1,0:T(2,128)S(1)}, f32[2,128]{1,0:T(2,128)S(1)}, u32[]{:S(2)}, u32[]{:S(2)}) %collective-permute-start.18) | collective-permute-done | bytes 1056 | tf_op jit(solution)/shard_map/ppermute | solution.py:411
  132.2 0.8 slice.103
  133.9 0.9 collective-permute-done.22
  135.9 11.6 %mix_adjoint.1 = (f32[2,17,32,128]{3,2,1,0:T(8,128)}, f32[2,64,512]{2,1,0:T(8,128)}, f32[2,64,512]{2,1,0:T(8,128)}, f32[2,64,512]{2,1,0:T(8,128)}, f32[2,64,512]{2,1,0:T(8,128)}) custom-call(f32[2,32,512]{2,1,0:T(8,128)} %bitcast.41, f32[4,32,512]{2,1,0:T(8,128)} %bitcast.63, f32[2,32,512]{2,1,0:T(8,128)} %bitcast.42, f32[4,32,512]{2,1,0:T(8,128)} %bitcast.64, ...), custom_call_target="tpu_custom_call" | custom-call | flops 9900000256 | bytes 31500000 | tf_op jit(solution)/shard_map/mix_adjoint/pallas_call | solution.py:466
  147.5 1.6 collective-permute-start.23
  149.1 1.5 collective-permute-start.27
  150.6 1.5 collective-permute-start.28
  152.6 1.4 collective-permute-start.24
  154.0 4.3 %collective-permute-done.23.refs_2_ = f32[2,8,8,512]{3,2,1,0:T(8,128)S(1)} collective-permute-done((f32[2,8,8,512]{3,2,1,0:T(8,128)}, f32[2,8,8,512]{3,2,1,0:T(8,128)S(1)}, u32[]{:S(2)}, u32[]{:S(2)}) %collective-permute-start.23) | collective-permute-done | bytes 262176 | tf_op jit(solution)/shard_map/ppermute | solution.py:411
  158.4 2.6 %collective-permute-start.25 = (f32[2,8,8,512]{3,2,1,0:T(8,128)}, f32[2,8,8,512]{3,2,1,0:T(8,128)S(1)}, u32[]{:S(2)}, u32[]{:S(2)}) collective-permute-start(f32[2,8,8,512]{3,2,1,0:T(8,128)} %bitcast.56), channel_id=1, source_target_pairs={{0,6},{1,7},{2,4},{3,5},{4,2},{5,3},{6,0},{7,1},{8,14},{9,15},{10,... | collective-permute-start | bytes 786440 | tf_op jit(solution)/shard_map/ppermute | solution.py:411
  160.9 0.9 slice_bitcast_fusion
  161.9 12.2 %collective-permute-done.24.refs_4_ = f32[2,8,8,512]{3,2,1,0:T(8,128)S(1)} collective-permute-done((f32[2,8,8,512]{3,2,1,0:T(8,128)}, f32[2,8,8,512]{3,2,1,0:T(8,128)S(1)}, u32[]{:S(2)}, u32[]{:S(2)}) %collective-permute-start.24) | collective-permute-done | bytes 262176 | tf_op jit(solution)/shard_map/ppermute | solution.py:411
  174.2 2.7 %collective-permute-done.28.refs_3_ = f32[2,17,32,128]{3,2,1,0:T(8,128)S(1)} collective-permute-done((f32[2,17,32,128]{3,2,1,0:T(8,128)}, f32[2,17,32,128]{3,2,1,0:T(8,128)S(1)}, u32[]{:S(2)}, u32[]{:S(2)}) %collective-permute-start.28) | collective-permute-done | bytes 557088 | tf_op jit(solution)/shard_map/ppermute | solution.py:442
  176.9 0.7 fusion
  178.3 9.3 %weight_gradient.1 = f32[2,16,16,4096]{3,2,1,0:T(8,128)} custom-call(f32[4,2,16,32,128]{4,3,2,1,0:T(8,128)} %bitcast.50, f32[2,17,32,128]{3,2,1,0:T(8,128)} %get-tuple-element.110.refs_1_, f32[2,17,32,128]{3,2,1,0:T(8,128)} %copy-done.18, f32[2,17,32,128]{3,2,1,0:T(8,128)} %copy-done.19, f32[2,17,32,128]{3,2,1,0:T(8,128)} %copy-done.20), custom_call_target="tpu_custom_call" | custom-call | flops 9900000256 | bytes 31500000 | tf_op jit(solution)/shard_map/weight_gradient/pallas_call | solution.py:591
  187.7 0.8 copy-done.21
  188.4 9.3 %input_gradient.1 = bf16[1,8,16,128,128]{4,3,2,1,0:T(8,128)(2,1)} custom-call(f32[2,8,8,512]{3,2,1,0:T(8,128)} %bitcast.33, f32[4,8,8,512]{3,2,1,0:T(8,128)} %copy-done.21, f32[2,8,8,512]{3,2,1,0:T(8,128)} %copy-done.1, f32[4,8,8,512]{3,2,1,0:T(8,128)} %copy-done.21, f32[2,8,8,512]{3,2,1,0:T(8,128)} %copy-done.2, f32[4,8,8,512]{3,2,1,0:T(8,128)} %copy-done.21, ...), custom_call_target="tpu_custom_call" | custom-call | flops 11000000512 | bytes 35000000 | tf_op jit(solution)/shard_map/input_gradient/pallas_call | solution.py:576
  (116 shorter events, 5.8 us)
Async XLA Ops:
  7.2 127.7 %all-gather.3.cloned.1.call-start = ((), (), s32[]{:S(2)}) async-start(), calls=%async_computation | async-start | bytes 2621440 | tf_op jit(solution)/shard_map/all_gather | solution.py:495
  14.2 14.4 %collective-permute-start = (f32[2,8,8,512]{3,2,1,0:T(8,128)}, f32[2,8,8,512]{3,2,1,0:T(8,128)S(1)}, u32[]{:S(2)}, u32[]{:S(2)}) collective-permute-start(f32[2,8,8,512]{3,2,1,0:T(8,128)} %get-tuple-element.59), channel_id=1, source_target_pairs={{0,2},{1,3},{2,0},{3,1},{4,6},{5,7},{6,4},{7,5},{8,10},{9,11},{10,... | collective-permute-start | bytes 786440 | tf_op jit(solution)/shard_map/ppermute | solution.py:411
  17.2 21.6 %collective-permute-start.1 = (f32[2,8,8,512]{3,2,1,0:T(8,128)}, f32[2,8,8,512]{3,2,1,0:T(8,128)S(1)}, u32[]{:S(2)}, u32[]{:S(2)}) collective-permute-start(f32[2,8,8,512]{3,2,1,0:T(8,128)} %get-tuple-element.60), channel_id=1, source_target_pairs={{0,4},{1,5},{2,6},{3,7},{4,0},{5,1},{6,2},{7,3},{8,12},{9,13},{10,... | collective-permute-start | bytes 786440 | tf_op jit(solution)/shard_map/ppermute | solution.py:411
  19.8 19.0 %collective-permute-start.2 = (f32[2,8,8,512]{3,2,1,0:T(8,128)}, f32[2,8,8,512]{3,2,1,0:T(8,128)S(1)}, u32[]{:S(2)}, u32[]{:S(2)}) collective-permute-start(f32[2,8,8,512]{3,2,1,0:T(8,128)} %get-tuple-element.61), channel_id=1, source_target_pairs={{0,6},{1,7},{2,4},{3,5},{4,2},{5,3},{6,0},{7,1},{8,14},{9,15},{10,... | collective-permute-start | bytes 786440 | tf_op jit(solution)/shard_map/ppermute | solution.py:411
  28.6 12.3 %copy-start.4 = (f32[2,8,8,512]{3,2,1,0:T(8,128)}, f32[2,8,8,512]{3,2,1,0:T(8,128)S(1)}, u32[]{:S(2)}) copy-start(f32[2,8,8,512]{3,2,1,0:T(8,128)S(1)} %collective-permute-done) | copy-start | bytes 786436
  38.9 2.0 collective-permute-start.3
  53.1 10.6 %collective-permute-start.4 = (f32[2,4,8,512]{3,2,1,0:T(8,128)}, f32[2,4,8,512]{3,2,1,0:T(8,128)S(1)}, u32[]{:S(2)}, u32[]{:S(2)}) collective-permute-start(f32[2,4,8,512]{3,2,1,0:T(8,128)} %bitcast.69), channel_id=1, source_target_pairs={{0,2},{1,3},{2,0},{3,1},{4,6},{5,7},{6,4},{7,5},{8,10},{9,11},{10,... | collective-permute-start | bytes 393224 | tf_op jit(solution)/shard_map/ppermute | solution.py:411
  57.9 13.1 %collective-permute-start.5 = (f32[2,4,8,512]{3,2,1,0:T(8,128)}, f32[2,4,8,512]{3,2,1,0:T(8,128)S(1)}, u32[]{:S(2)}, u32[]{:S(2)}) collective-permute-start(f32[2,4,8,512]{3,2,1,0:T(8,128)} %bitcast.68), channel_id=1, source_target_pairs={{0,4},{1,5},{2,6},{3,7},{4,0},{5,1},{6,2},{7,3},{8,12},{9,13},{10,... | collective-permute-start | bytes 393224 | tf_op jit(solution)/shard_map/ppermute | solution.py:411
  58.9 12.0 %collective-permute-start.6 = (f32[2,4,8,512]{3,2,1,0:T(8,128)}, f32[2,4,8,512]{3,2,1,0:T(8,128)S(1)}, u32[]{:S(2)}, u32[]{:S(2)}) collective-permute-start(f32[2,4,8,512]{3,2,1,0:T(8,128)} %bitcast.67), channel_id=1, source_target_pairs={{0,6},{1,7},{2,4},{3,5},{4,2},{5,3},{6,0},{7,1},{8,14},{9,15},{10,... | collective-permute-start | bytes 393224 | tf_op jit(solution)/shard_map/ppermute | solution.py:411
  60.3 10.8 %collective-permute-start.8 = (f32[4,4,8,512]{3,2,1,0:T(8,128)}, f32[4,4,8,512]{3,2,1,0:T(8,128)S(1)}, u32[]{:S(2)}, u32[]{:S(2)}) collective-permute-start(f32[4,4,8,512]{3,2,1,0:T(8,128)} %bitcast.55), channel_id=1, source_target_pairs={{0,1},{1,0},{2,3},{3,2},{4,5},{5,4},{6,7},{7,6},{8,9},{9,8},{10,11... | collective-permute-start | bytes 786440 | tf_op jit(solution)/shard_map/ppermute | solution.py:411
  63.8 14.9 %copy-start.14 = (f32[2,4,8,512]{3,2,1,0:T(8,128)}, f32[2,4,8,512]{3,2,1,0:T(8,128)S(1)}, u32[]{:S(2)}) copy-start(f32[2,4,8,512]{3,2,1,0:T(8,128)S(1)} %collective-permute-done.4.refs_2_) | copy-start | bytes 393220
  71.0 7.7 %copy-start.15 = (f32[2,4,8,512]{3,2,1,0:T(8,128)}, f32[2,4,8,512]{3,2,1,0:T(8,128)S(1)}, u32[]{:S(2)}) copy-start(f32[2,4,8,512]{3,2,1,0:T(8,128)S(1)} %collective-permute-done.5.refs_4_) | copy-start | bytes 393220
  71.0 7.7 %copy-start.16 = (f32[2,4,8,512]{3,2,1,0:T(8,128)}, f32[2,4,8,512]{3,2,1,0:T(8,128)S(1)}, u32[]{:S(2)}) copy-start(f32[2,4,8,512]{3,2,1,0:T(8,128)S(1)} %collective-permute-done.6.refs_6_) | copy-start | bytes 393220
  71.0 7.6 %collective-permute-start.7 = (f32[4,4,8,512]{3,2,1,0:T(8,128)S(1)}, f32[4,4,8,512]{3,2,1,0:T(8,128)S(1)}, u32[]{:S(2)}, u32[]{:S(2)}) collective-permute-start(f32[4,4,8,512]{3,2,1,0:T(8,128)S(1)} %pad_maximum_fusion.2), channel_id=1, source_target_pairs={{0,1},{1,0},{2,3},{3,2},{4,5},{5,4},{6,7},{7,6},{8,9},{9,8},{10,11... | collective-permute-start | bytes 786440 | tf_op jit(solution)/shard_map/ppermute | solution.py:411
  71.1 24.5 %copy-start = (f32[4,4,8,512]{3,2,1,0:T(8,128)}, f32[4,4,8,512]{3,2,1,0:T(8,128)S(1)}, u32[]{:S(2)}) copy-start(f32[4,4,8,512]{3,2,1,0:T(8,128)S(1)} %collective-permute-done.8.refs_1_) | copy-start | bytes 786436
  72.1 23.6 %collective-permute-start.10 = (f32[2,4,8,512]{3,2,1,0:T(8,128)S(1)}, f32[2,4,8,512]{3,2,1,0:T(8,128)S(1)}, u32[]{:S(2)}, u32[]{:S(2)}) collective-permute-start(f32[2,4,8,512]{3,2,1,0:T(8,128)S(1)} %pad_maximum_fusion.6), channel_id=1, source_target_pairs={{0,4},{1,5},{2,6},{3,7},{4,0},{5,1},{6,2},{7,3},{8,12},{9,13},{10,... | collective-permute-start | bytes 393224 | tf_op jit(solution)/shard_map/ppermute | solution.py:411
  76.2 19.5 %collective-permute-start.11 = (f32[2,4,8,512]{3,2,1,0:T(8,128)S(1)}, f32[2,4,8,512]{3,2,1,0:T(8,128)S(1)}, u32[]{:S(2)}, u32[]{:S(2)}) collective-permute-start(f32[2,4,8,512]{3,2,1,0:T(8,128)S(1)} %pad_maximum_fusion.7), channel_id=1, source_target_pairs={{0,6},{1,7},{2,4},{3,5},{4,2},{5,3},{6,0},{7,1},{8,14},{9,15},{10,... | collective-permute-start | bytes 393224 | tf_op jit(solution)/shard_map/ppermute | solution.py:411
  78.6 17.2 %collective-permute-start.9 = (f32[2,4,8,512]{3,2,1,0:T(8,128)S(1)}, f32[2,4,8,512]{3,2,1,0:T(8,128)S(1)}, u32[]{:S(2)}, u32[]{:S(2)}) collective-permute-start(f32[2,4,8,512]{3,2,1,0:T(8,128)S(1)} %pad_maximum_fusion.5), channel_id=1, source_target_pairs={{0,2},{1,3},{2,0},{3,1},{4,6},{5,7},{6,4},{7,5},{8,10},{9,11},{10,... | collective-permute-start | bytes 393224 | tf_op jit(solution)/shard_map/ppermute | solution.py:411
  95.7 4.6 %copy-start.26 = (f32[2,4,8,512]{3,2,1,0:T(8,128)}, f32[2,4,8,512]{3,2,1,0:T(8,128)S(1)}, u32[]{:S(2)}) copy-start(f32[2,4,8,512]{3,2,1,0:T(8,128)S(1)} %collective-permute-done.10.refs_4_.refs_5_) | copy-start | bytes 393220
  95.7 4.6 %copy-start.27 = (f32[2,4,8,512]{3,2,1,0:T(8,128)}, f32[2,4,8,512]{3,2,1,0:T(8,128)S(1)}, u32[]{:S(2)}) copy-start(f32[2,4,8,512]{3,2,1,0:T(8,128)S(1)} %collective-permute-done.11.refs_6_.refs_7_) | copy-start | bytes 393220
  95.7 4.6 %copy-start.28 = (f32[2,4,8,512]{3,2,1,0:T(8,128)}, f32[2,4,8,512]{3,2,1,0:T(8,128)S(1)}, u32[]{:S(2)}) copy-start(f32[2,4,8,512]{3,2,1,0:T(8,128)S(1)} %collective-permute-done.9.refs_2_.refs_3_) | copy-start | bytes 393220
  95.8 21.2 %collective-permute-start.12 = (f32[2,4,8,512]{3,2,1,0:T(8,128)}, f32[2,4,8,512]{3,2,1,0:T(8,128)S(1)}, u32[]{:S(2)}, u32[]{:S(2)}) collective-permute-start(f32[2,4,8,512]{3,2,1,0:T(8,128)} %get-tuple-element.88), channel_id=1, source_target_pairs={{0,2},{1,3},{2,0},{3,1},{4,6},{5,7},{6,4},{7,5},{8,10},{9,11},{10,... | collective-permute-start | bytes 393224 | tf_op jit(solution)/shard_map/ppermute | solution.py:411
  97.9 19.1 %collective-permute-start.13 = (f32[2,4,8,512]{3,2,1,0:T(8,128)}, f32[2,4,8,512]{3,2,1,0:T(8,128)S(1)}, u32[]{:S(2)}, u32[]{:S(2)}) collective-permute-start(f32[2,4,8,512]{3,2,1,0:T(8,128)} %get-tuple-element.89), channel_id=1, source_target_pairs={{0,4},{1,5},{2,6},{3,7},{4,0},{5,1},{6,2},{7,3},{8,12},{9,13},{10,... | collective-permute-start | bytes 393224 | tf_op jit(solution)/shard_map/ppermute | solution.py:411
  98.9 18.1 %collective-permute-start.14 = (f32[2,4,8,512]{3,2,1,0:T(8,128)}, f32[2,4,8,512]{3,2,1,0:T(8,128)S(1)}, u32[]{:S(2)}, u32[]{:S(2)}) collective-permute-start(f32[2,4,8,512]{3,2,1,0:T(8,128)} %get-tuple-element.90), channel_id=1, source_target_pairs={{0,6},{1,7},{2,4},{3,5},{4,2},{5,3},{6,0},{7,1},{8,14},{9,15},{10,... | collective-permute-start | bytes 393224 | tf_op jit(solution)/shard_map/ppermute | solution.py:411
  100.3 21.2 %copy-start.17 = (f32[16,16]{1,0:T(8,128)S(1)}, f32[16,16]{1,0:T(8,128)}, u32[]{:S(2)}) copy-start(f32[16,16]{1,0:T(8,128)} %get-tuple-element.96) | copy-start | bytes 3076
  100.3 32.8 %copy-start.7 = (f32[2,4,8,512]{3,2,1,0:T(8,128)S(1)}, f32[2,4,8,512]{3,2,1,0:T(8,128)}, u32[]{:S(2)}) copy-start(f32[2,4,8,512]{3,2,1,0:T(8,128)} %get-tuple-element.91) | copy-start | bytes 393220
  117.0 18.3 %copy-start.8 = (f32[2,4,8,512]{3,2,1,0:T(8,128)}, f32[2,4,8,512]{3,2,1,0:T(8,128)S(1)}, u32[]{:S(2)}) copy-start(f32[2,4,8,512]{3,2,1,0:T(8,128)S(1)} %collective-permute-done.12) | copy-start | bytes 393220
  117.0 18.2 %copy-start.9 = (f32[2,4,8,512]{3,2,1,0:T(8,128)}, f32[2,4,8,512]{3,2,1,0:T(8,128)S(1)}, u32[]{:S(2)}) copy-start(f32[2,4,8,512]{3,2,1,0:T(8,128)S(1)} %collective-permute-done.13) | copy-start | bytes 393220
  117.0 18.2 %copy-start.10 = (f32[2,4,8,512]{3,2,1,0:T(8,128)}, f32[2,4,8,512]{3,2,1,0:T(8,128)S(1)}, u32[]{:S(2)}) copy-start(f32[2,4,8,512]{3,2,1,0:T(8,128)S(1)} %collective-permute-done.14) | copy-start | bytes 393220
  117.0 16.1 %collective-permute-start.19 = (f32[2,4,8,512]{3,2,1,0:T(8,128)}, f32[2,4,8,512]{3,2,1,0:T(8,128)S(1)}, u32[]{:S(2)}, u32[]{:S(2)}) collective-permute-start(f32[2,4,8,512]{3,2,1,0:T(8,128)} %get-tuple-element.99), channel_id=1, source_target_pairs={{0,2},{1,3},{2,0},{3,1},{4,6},{5,7},{6,4},{7,5},{8,10},{9,11},{10,... | collective-permute-start | bytes 393224 | tf_op jit(solution)/shard_map/ppermute | solution.py:411
  118.2 15.0 %collective-permute-start.20 = (f32[2,4,8,512]{3,2,1,0:T(8,128)}, f32[2,4,8,512]{3,2,1,0:T(8,128)S(1)}, u32[]{:S(2)}, u32[]{:S(2)}) collective-permute-start(f32[2,4,8,512]{3,2,1,0:T(8,128)} %get-tuple-element.100), channel_id=1, source_target_pairs={{0,4},{1,5},{2,6},{3,7},{4,0},{5,1},{6,2},{7,3},{8,12},{9,13},{10,... | collective-permute-start | bytes 393224 | tf_op jit(solution)/shard_map/ppermute | solution.py:411
  120.1 13.1 %collective-permute-start.21 = (f32[2,4,8,512]{3,2,1,0:T(8,128)}, f32[2,4,8,512]{3,2,1,0:T(8,128)S(1)}, u32[]{:S(2)}, u32[]{:S(2)}) collective-permute-start(f32[2,4,8,512]{3,2,1,0:T(8,128)} %get-tuple-element.101), channel_id=1, source_target_pairs={{0,6},{1,7},{2,4},{3,5},{4,2},{5,3},{6,0},{7,1},{8,14},{9,15},{10,... | collective-permute-start | bytes 393224 | tf_op jit(solution)/shard_map/ppermute | solution.py:411
  122.3 1.1 collective-permute-start.16
  123.4 3.6 %collective-permute-start.17 = (f32[2,128]{1,0:T(2,128)S(1)}, f32[2,128]{1,0:T(2,128)S(1)}, u32[]{:S(2)}, u32[]{:S(2)}) collective-permute-start(f32[2,128]{1,0:T(2,128)S(1)} %add.28), channel_id=1, source_target_pairs={{0,2},{1,3},{2,0},{3,1},{4,6},{5,7},{6,4},{7,5},{8,10},{9,11},{10,... | collective-permute-start | bytes 3080 | tf_op jit(solution)/shard_map/ppermute | solution.py:411
  127.0 4.7 %collective-permute-start.18 = (f32[2,128]{1,0:T(2,128)S(1)}, f32[2,128]{1,0:T(2,128)S(1)}, u32[]{:S(2)}, u32[]{:S(2)}) collective-permute-start(f32[2,128]{1,0:T(2,128)S(1)} %add.29), channel_id=1, source_target_pairs={{0,4},{1,5},{2,6},{3,7},{4,0},{5,1},{6,2},{7,3},{8,12},{9,13},{10,... | collective-permute-start | bytes 3080 | tf_op jit(solution)/shard_map/ppermute | solution.py:411
  133.2 1.6 collective-permute-start.22
  133.4 1.9 collective-permute-start.15
  147.5 10.9 %collective-permute-start.23 = (f32[2,8,8,512]{3,2,1,0:T(8,128)}, f32[2,8,8,512]{3,2,1,0:T(8,128)S(1)}, u32[]{:S(2)}, u32[]{:S(2)}) collective-permute-start(f32[2,8,8,512]{3,2,1,0:T(8,128)} %bitcast.62), channel_id=1, source_target_pairs={{0,2},{1,3},{2,0},{3,1},{4,6},{5,7},{6,4},{7,5},{8,10},{9,11},{10,... | collective-permute-start | bytes 786440 | tf_op jit(solution)/shard_map/ppermute | solution.py:411
  149.1 25.1 %collective-permute-start.27 = (f32[2,17,32,128]{3,2,1,0:T(8,128)}, f32[2,17,32,128]{3,2,1,0:T(8,128)S(1)}, u32[]{:S(2)}, u32[]{:S(2)}) collective-permute-start(f32[2,17,32,128]{3,2,1,0:T(8,128)} %get-tuple-element.110.refs_1_), channel_id=1, source_target_pairs={{0,8},{8,0},{16,24},{24,16},{1,9},{9,1},{17,25},{25,17},{2,10},{10... | collective-permute-start | bytes 1671176 | tf_op jit(solution)/shard_map/ppermute | solution.py:442
  150.6 26.3 %collective-permute-start.28 = (f32[2,17,32,128]{3,2,1,0:T(8,128)}, f32[2,17,32,128]{3,2,1,0:T(8,128)S(1)}, u32[]{:S(2)}, u32[]{:S(2)}) collective-permute-start(f32[2,17,32,128]{3,2,1,0:T(8,128)} %get-tuple-element.110.refs_1_), channel_id=1, source_target_pairs={{0,16},{8,24},{16,0},{24,8},{1,17},{9,25},{17,1},{25,9},{2,18},{10... | collective-permute-start | bytes 1671176 | tf_op jit(solution)/shard_map/ppermute | solution.py:442
  152.1 24.8 %collective-permute-start.29 = (f32[2,17,32,128]{3,2,1,0:T(8,128)}, f32[2,17,32,128]{3,2,1,0:T(8,128)S(1)}, u32[]{:S(2)}, u32[]{:S(2)}) collective-permute-start(f32[2,17,32,128]{3,2,1,0:T(8,128)} %get-tuple-element.110.refs_1_), channel_id=1, source_target_pairs={{0,24},{8,16},{16,8},{24,0},{1,25},{9,17},{17,9},{25,1},{2,26},{10... | collective-permute-start | bytes 1671176 | tf_op jit(solution)/shard_map/ppermute | solution.py:442
  152.6 21.4 %collective-permute-start.24 = (f32[2,8,8,512]{3,2,1,0:T(8,128)}, f32[2,8,8,512]{3,2,1,0:T(8,128)S(1)}, u32[]{:S(2)}, u32[]{:S(2)}) collective-permute-start(f32[2,8,8,512]{3,2,1,0:T(8,128)} %bitcast.57), channel_id=1, source_target_pairs={{0,4},{1,5},{2,6},{3,7},{4,0},{5,1},{6,2},{7,3},{8,12},{9,13},{10,... | collective-permute-start | bytes 786440 | tf_op jit(solution)/shard_map/ppermute | solution.py:411
  158.4 29.3 %copy-start.1 = (f32[2,8,8,512]{3,2,1,0:T(8,128)}, f32[2,8,8,512]{3,2,1,0:T(8,128)S(1)}, u32[]{:S(2)}) copy-start(f32[2,8,8,512]{3,2,1,0:T(8,128)S(1)} %collective-permute-done.23.refs_2_) | copy-start | bytes 786436
  158.4 15.7 %collective-permute-start.25 = (f32[2,8,8,512]{3,2,1,0:T(8,128)}, f32[2,8,8,512]{3,2,1,0:T(8,128)S(1)}, u32[]{:S(2)}, u32[]{:S(2)}) collective-permute-start(f32[2,8,8,512]{3,2,1,0:T(8,128)} %bitcast.56), channel_id=1, source_target_pairs={{0,6},{1,7},{2,4},{3,5},{4,2},{5,3},{6,0},{7,1},{8,14},{9,15},{10,... | collective-permute-start | bytes 786440 | tf_op jit(solution)/shard_map/ppermute | solution.py:411
  174.0 13.6 %copy-start.2 = (f32[2,8,8,512]{3,2,1,0:T(8,128)}, f32[2,8,8,512]{3,2,1,0:T(8,128)S(1)}, u32[]{:S(2)}) copy-start(f32[2,8,8,512]{3,2,1,0:T(8,128)S(1)} %collective-permute-done.24.refs_4_) | copy-start | bytes 786436
  174.0 13.6 %copy-start.3 = (f32[2,8,8,512]{3,2,1,0:T(8,128)}, f32[2,8,8,512]{3,2,1,0:T(8,128)S(1)}, u32[]{:S(2)}) copy-start(f32[2,8,8,512]{3,2,1,0:T(8,128)S(1)} %collective-permute-done.25.refs_6_) | copy-start | bytes 786436
  174.1 13.5 %collective-permute-start.26 = (f32[4,8,8,512]{3,2,1,0:T(8,128)S(1)}, f32[4,8,8,512]{3,2,1,0:T(8,128)S(1)}, u32[]{:S(2)}, u32[]{:S(2)}) collective-permute-start(f32[4,8,8,512]{3,2,1,0:T(8,128)S(1)} %pad_maximum_fusion.1), channel_id=1, source_target_pairs={{0,1},{1,0},{2,3},{3,2},{4,5},{5,4},{6,7},{7,6},{8,9},{9,8},{10,11... | collective-permute-start | bytes 1572872 | tf_op jit(solution)/shard_map/ppermute | solution.py:411
  174.2 4.1 %copy-start.18 = (f32[2,17,32,128]{3,2,1,0:T(8,128)}, f32[2,17,32,128]{3,2,1,0:T(8,128)S(1)}, u32[]{:S(2)}) copy-start(f32[2,17,32,128]{3,2,1,0:T(8,128)S(1)} %collective-permute-done.27.refs_2_) | copy-start | bytes 1671172
  (12 other events, 16.9 us)
Sparse Core Ops, SparseCore 0:
  60.5 35.5 all-gather.2

commit v3 on v2

--- a/solution.py
+++ b/solution.py
@@ -359,7 +359,7 @@
             out_ref[1, c, :, lanes] = imag
 
 
-def params(steps, megabytes=60):
+def params(steps, megabytes=24):
     return pltpu.CompilerParams(
         dimension_semantics=("arbitrary",) * steps, vmem_limit_bytes=megabytes * 1024 * 1024
     )
@@ -470,7 +470,7 @@
             out_specs=[whole_spec(made)] + [whole_spec(v) for v in outs],
             out_shape=[made] + outs,
             scratch_shapes=[pltpu.VMEM(spec_shape.shape, F32), pltpu.VMEM((groups, near * rows, wide), F32)],
-            compiler_params=params(1),
+            compiler_params=params(1, 24),
             name=name,
             cost_estimate=cost(9),
         )(*operands, *constants)
@@ -490,8 +490,8 @@
     )(fields, tab["y_fwd"], tab["x_fwd"])
     arrived = [swap_last(forward)]
 
-    u_spec, mixed = mix_call(mix_kernel, "mix_modes", arrived, (False, True), scale)
-    planes = [swap_last(mixed[0]), swap_first(mixed[1])]
+    u_spec, mixed = mix_call(mix_kernel, "mix_modes", arrived, (False,) * cut_out, scale)
+    planes = [cross(m) for m in mixed]
     u_all = lax.all_gather(u_spec, "dp")
 
     side = channels * GROUP
@@ -540,10 +540,8 @@
     act, points, arrived = None, [], []
     for h in range(cut_out):
         if h:
-            point, values = lax.optimization_barrier((points[-1], [v for v, _ in planes[h]]))
-            points[-1] = point
-            planes[h] = [(v, lead) for v, (_, lead) in zip(values, planes[h])]
-        layer_output, part, point, *blocks = middle(h, planes[h], act)
+            points[-1], planes[h] = lax.optimization_barrier((points[-1], planes[h]))
+        layer_output, part, point, *blocks = middle(h, swap(planes[h]), act)
         act = [layer_output, part]
         points.append(point)
         if h:

time: 205 us -> 196 us (0.956)
  Pallas kernels: 81.6 us -> 61.6 us
  local copies, waits for them, and re-layouts: 7.38 us -> 19.9 us
  other arithmetic: 4.75 us -> 1.67 us
  waiting for transfers between devices: 57.2 us -> 59.4 us
    unnamed x58 -> x42, local copies, waits for them, and re-layouts: 2.97 us -> 18.9 us
    pallas_call x2, Pallas kernels: 23.1 us -> 13.4 us  [mix_call(): pl.pallas_call(functools.partial(kernel, len(operands), len(outs), first,...]
    pallas_call x2, Pallas kernels: 33 us -> 28.1 us  [middle(): pl.pallas_call(body, grid=(part_near,), in_specs=in_specs, out_specs=[her...]
    slice x20 -> x24, local copies, waits for them, and re-layouts: 3.64 us -> 0.17 us  [swap(): swapped = hop(jnp.stack([g[1] for g in got]), 1)]
    ppermute x27, waiting for transfers between devices: 54.5 us -> 57.5 us  [hop(): return lax.ppermute(values, 'gz', [(i, i ^ j) for i in range(groups)])]
    concatenate x3 -> x0, other arithmetic: 2.63 us -> none  [swap_first(): got[c] = hop(jnp.concatenate([near_blocks[c], swapped[c:c + 1]]), CORES * c)]
    pallas_call x1, Pallas kernels: 6.95 us -> 4.59 us  [shards(): pl.pallas_call(fields_kernel, grid=(near // batch,), in_specs=[plane, who...]
  transfers between devices with their start and end apart: 31 -> 31, of which waited for: 13 -> 13; matrix products, arithmetic and copies ran while one was open for 4% -> 1% of each run, Pallas kernels for 21% -> 19%
where the time goes in v3:
time: 196 us; the launch traced here: 195 us
  Pallas kernels  61.6 us (31%)
  waiting for transfers between devices  59.4 us (30%)
  starting transfers between devices  37.9 us (19%)
  local copies, waits for them, and re-layouts  19.9 us (10%)
  between operations  14.4 us (7%)
    ppermute x27, waiting for transfers between devices, hop(): return lax.ppermute(values, 'gz', [(i, i ^ j) for i in range(groups)])  57.5 us
    ppermute x27, starting transfers between devices, hop(): return lax.ppermute(values, 'gz', [(i, i ^ j) for i in range(groups)])  34.4 us
    pallas_call x2, Pallas kernels, middle(): pl.pallas_call(body, grid=(part_near,), in_specs=in_specs, out_specs=[her...  28.1 us
    unnamed x42, local copies, waits for them, and re-layouts  18.9 us
    pallas_call x2, Pallas kernels, mix_call(): pl.pallas_call(functools.partial(kernel, len(operands), len(outs), first,...  13.4 us
    pallas_call x1, Pallas kernels, shards(): pl.pallas_call(functools.partial(weight_grad_kernel, math.sqrt(total_mode...  8.12 us
    pallas_call x1, Pallas kernels, shards(): pl.pallas_call(functools.partial(final_kernel, groups), grid=(near // bat...  7.29 us
    pallas_call x1, Pallas kernels, shards(): pl.pallas_call(fields_kernel, grid=(near // batch,), in_specs=[plane, who...  4.59 us
  transfers between devices with their start and end apart: 31, of which 13 were waited for; matrix products, arithmetic and copies ran while one was open for 1% of the time, Pallas kernels for 19%

profile of v3, /device:TPU:0, one launch (start us, length us, event | category | flops | bytes accessed | tf_op | source)
XLA Modules:
  0.0 194.9 jit_solution(13775959076018190364)
XLA Ops:
  7.2 2.2 %copy-done = bf16[1,8,16,128,128]{4,3,2,1,0:T(8,128)(2,1)S(1)} copy-done((bf16[1,8,16,128,128]{4,3,2,1,0:T(8,128)(2,1)S(1)}, bf16[1,8,16,128,128]{4,3,2,1,0:T(8,128)(2,1)}, u32[]{:S(2)}) %copy-start) | copy-done | bytes 4194328
  9.4 1.1 copy-done.12
  10.5 0.8 copy-done.16
  11.4 4.6 %fields_forward.1 = (f32[2,8,8,512]{3,2,1,0:T(8,128)S(1)}, f32[2,8,8,512]{3,2,1,0:T(8,128)S(1)}, f32[2,8,8,512]{3,2,1,0:T(8,128)S(1)}, f32[2,8,8,512]{3,2,1,0:T(8,128)S(1)}) custom-call(bf16[1,8,16,128,128]{4,3,2,1,0:T(8,128)(2,1)S(1)} %copy-done, bf16[1536,256]{1,0:T(8,128)(2,1)S(1)} %copy-done.12, bf16[128,256]{1,0:T(8,128)(2,1)S(1)} %copy-done.16), custom_call_target="tpu_custom_call" | custom-call | flops 5500000256 | bytes 17500000 | tf_op jit(solution)/shard_map/fields_forward/pallas_call | solution.py:480
  16.0 3.1 %collective-permute-start = (f32[2,8,8,512]{3,2,1,0:T(8,128)S(1)}, f32[2,8,8,512]{3,2,1,0:T(8,128)S(1)}, u32[]{:S(2)}, u32[]{:S(2)}) collective-permute-start(f32[2,8,8,512]{3,2,1,0:T(8,128)S(1)} %get-tuple-element.54), channel_id=1, source_target_pairs={{0,2},{1,3},{2,0},{3,1},{4,6},{5,7},{6,4},{7,5},{8,10},{9,11},{10,... | collective-permute-start | bytes 786440 | tf_op jit(solution)/shard_map/ppermute | solution.py:411
  19.1 2.6 %collective-permute-start.1 = (f32[2,8,8,512]{3,2,1,0:T(8,128)S(1)}, f32[2,8,8,512]{3,2,1,0:T(8,128)S(1)}, u32[]{:S(2)}, u32[]{:S(2)}) collective-permute-start(f32[2,8,8,512]{3,2,1,0:T(8,128)S(1)} %get-tuple-element.55), channel_id=1, source_target_pairs={{0,4},{1,5},{2,6},{3,7},{4,0},{5,1},{6,2},{7,3},{8,12},{9,13},{10,... | collective-permute-start | bytes 786440 | tf_op jit(solution)/shard_map/ppermute | solution.py:411
  21.7 8.5 %collective-permute-done = f32[2,8,8,512]{3,2,1,0:T(8,128)S(1)} collective-permute-done((f32[2,8,8,512]{3,2,1,0:T(8,128)S(1)}, f32[2,8,8,512]{3,2,1,0:T(8,128)S(1)}, u32[]{:S(2)}, u32[]{:S(2)}) %collective-permute-start) | collective-permute-done | bytes 262176 | tf_op jit(solution)/shard_map/ppermute | solution.py:411
  30.2 10.2 %collective-permute-done.1 = f32[2,8,8,512]{3,2,1,0:T(8,128)S(1)} collective-permute-done((f32[2,8,8,512]{3,2,1,0:T(8,128)S(1)}, f32[2,8,8,512]{3,2,1,0:T(8,128)S(1)}, u32[]{:S(2)}, u32[]{:S(2)}) %collective-permute-start.1) | collective-permute-done | bytes 262176 | tf_op jit(solution)/shard_map/ppermute | solution.py:411
  40.6 1.9 collective-permute-done.3
  42.6 6.7 %mix_modes.1 = (f32[2,16,32,128]{3,2,1,0:T(8,128)}, f32[2,32,512]{2,1,0:T(8,128)S(1)}, f32[2,32,512]{2,1,0:T(8,128)S(1)}, f32[2,32,512]{2,1,0:T(8,128)S(1)}, f32...) custom-call(f32[2,64,512]{2,1,0:T(8,128)S(1)} %bitcast.33, ...), custom_call_target="tpu_custom_call" | custom-call | flops 9900000256 | bytes 31500000 | tf_op jit(solution)/shard_map/mix_modes/pallas_call | solution.py:466
  49.3 4.8 %collective-permute-start.4 = (f32[2,4,8,512]{3,2,1,0:T(8,128)S(1)}, f32[2,4,8,512]{3,2,1,0:T(8,128)S(1)}, u32[]{:S(2)}, u32[]{:S(2)}) collective-permute-start(f32[2,4,8,512]{3,2,1,0:T(8,128)S(1)} %bitcast.69), channel_id=1, source_target_pairs={{0,2},{1,3},{2,0},{3,1},{4,6},{5,7},{6,4},{7,5},{8,10},{9,11},{10,... | collective-permute-start | bytes 393224 | tf_op jit(solution)/shard_map/ppermute | solution.py:411
  54.0 1.1 collective-permute-start.5
  55.2 1.4 collective-permute-start.6
  56.6 3.2 %collective-permute-done.4.refs_2_ = f32[2,4,8,512]{3,2,1,0:T(8,128)S(1)} collective-permute-done((f32[2,4,8,512]{3,2,1,0:T(8,128)S(1)}, f32[2,4,8,512]{3,2,1,0:T(8,128)S(1)}, u32[]{:S(2)}, u32[]{:S(2)}) %collective-permute-start.4) | collective-permute-done | bytes 131104 | tf_op jit(solution)/shard_map/ppermute | solution.py:411
  59.7 7.2 %collective-permute-done.5.refs_4_ = f32[2,4,8,512]{3,2,1,0:T(8,128)S(1)} collective-permute-done((f32[2,4,8,512]{3,2,1,0:T(8,128)S(1)}, f32[2,4,8,512]{3,2,1,0:T(8,128)S(1)}, u32[]{:S(2)}, u32[]{:S(2)}) %collective-permute-start.5) | collective-permute-done | bytes 131104 | tf_op jit(solution)/shard_map/ppermute | solution.py:411
  67.7 2.3 %collective-permute-start.10 = (f32[2,4,8,512]{3,2,1,0:T(8,128)S(1)}, f32[2,4,8,512]{3,2,1,0:T(8,128)S(1)}, u32[]{:S(2)}, u32[]{:S(2)}) collective-permute-start(f32[2,4,8,512]{3,2,1,0:T(8,128)S(1)} %bitcast.66), channel_id=1, source_target_pairs={{0,6},{1,7},{2,4},{3,5},{4,2},{5,3},{6,0},{7,1},{8,14},{9,15},{10,... | collective-permute-start | bytes 393224 | tf_op jit(solution)/shard_map/ppermute | solution.py:411
  70.0 1.6 collective-permute-start.8
  72.2 2.2 %copy-done.1 = bf16[1,8,16,128,128]{4,3,2,1,0:T(8,128)(2,1)S(1)} copy-done((bf16[1,8,16,128,128]{4,3,2,1,0:T(8,128)(2,1)S(1)}, bf16[1,8,16,128,128]{4,3,2,1,0:T(8,128)(2,1)}, u32[]{:S(2)}) %copy-start.1) | copy-done | bytes 4194328
  74.4 2.2 %copy-done.2 = bf16[1,8,16,128,128]{4,3,2,1,0:T(8,128)(2,1)S(1)} copy-done((bf16[1,8,16,128,128]{4,3,2,1,0:T(8,128)(2,1)S(1)}, bf16[1,8,16,128,128]{4,3,2,1,0:T(8,128)(2,1)}, u32[]{:S(2)}) %copy-start.2) | copy-done | bytes 4194328
  76.6 0.8 copy-done.17
  77.4 0.8 copy-done.18
  78.2 14.0 %middle0.1 = (bf16[1,8,16,128,128]{4,3,2,1,0:T(8,128)(2,1)}, f32[8,16,128,128]{3,2,1,0:T(8,128)S(1)}, f32[16,16]{1,0:T(8,128)S(1)}, f32[2,4,8,512]{3,2,1,0:T(8,1...) custom-call(f32[2,4,8,512]{3,2,1,0:T(8,128)S(1)} %bitcast.47, ...), custom_call_target="tpu_custom_call" | custom-call | flops 19800000512 | bytes 63000000 | tf_op jit(solution)/shard_map/middle0/pallas_call | solution.py:520
  92.4 1.5 collective-permute-start.12
  93.9 1.5 collective-permute-start.13
  95.4 1.5 collective-permute-start.14
  96.9 14.1 %middle1.1 = (bf16[1,8,16,128,128]{4,3,2,1,0:T(8,128)(2,1)}, f32[8,16,128,128]{3,2,1,0:T(8,128)S(1)}, f32[16,16]{1,0:T(8,128)S(1)}, f32[2,4,8,512]{3,2,1,0:T(8,1...) custom-call(f32[2,4,8,512]{3,2,1,0:T(8,128)S(1)} %bitcast.43, ...), custom_call_target="tpu_custom_call", output_to_operand_aliasing={{0}: (16, {}), {1}: (17, {})} | custom-call | flops 19800000512 | bytes 63000000 | tf_op jit(solution)/shard_map/middle1/pallas_call | solution.py:520
  111.0 3.3 %copy-done.19 = f32[8,16,128,128]{3,2,1,0:T(8,128)} copy-done((f32[8,16,128,128]{3,2,1,0:T(8,128)}, f32[8,16,128,128]{3,2,1,0:T(8,128)S(1)}, u32[]{:S(2)}) %copy-start.19) | copy-done | bytes 8388632
  114.9 2.4 %collective-permute-start.20 = (f32[2,4,8,512]{3,2,1,0:T(8,128)S(1)}, f32[2,4,8,512]{3,2,1,0:T(8,128)S(1)}, u32[]{:S(2)}, u32[]{:S(2)}) collective-permute-start(f32[2,4,8,512]{3,2,1,0:T(8,128)S(1)} %get-tuple-element.90), channel_id=1, source_target_pairs={{0,4},{1,5},{2,6},{3,7},{4,0},{5,1},{6,2},{7,3},{8,12},{9,13},{10,... | collective-permute-start | bytes 393224 | tf_op jit(solution)/shard_map/ppermute | solution.py:411
  117.3 1.5 collective-permute-start.21
  118.9 1.1 collective-permute-done.16
  120.0 3.6 %collective-permute-done.17 = f32[2,128]{1,0:T(2,128)S(1)} collective-permute-done((f32[2,128]{1,0:T(2,128)S(1)}, f32[2,128]{1,0:T(2,128)S(1)}, u32[]{:S(2)}, u32[]{:S(2)}) %collective-permute-start.17) | collective-permute-done | bytes 1056 | tf_op jit(solution)/shard_map/ppermute | solution.py:411
  123.6 3.0 %collective-permute-start.18 = (f32[2,128]{1,0:T(2,128)S(1)}, f32[2,128]{1,0:T(2,128)S(1)}, u32[]{:S(2)}, u32[]{:S(2)}) collective-permute-start(f32[2,128]{1,0:T(2,128)S(1)} %add.29), channel_id=1, source_target_pairs={{0,4},{1,5},{2,6},{3,7},{4,0},{5,1},{6,2},{7,3},{8,12},{9,13},{10,... | collective-permute-start | bytes 3080 | tf_op jit(solution)/shard_map/ppermute | solution.py:411
  126.6 2.4 %collective-permute-done.18 = f32[2,128]{1,0:T(2,128)S(1)} collective-permute-done((f32[2,128]{1,0:T(2,128)S(1)}, f32[2,128]{1,0:T(2,128)S(1)}, u32[]{:S(2)}, u32[]{:S(2)}) %collective-permute-start.18) | collective-permute-done | bytes 1056 | tf_op jit(solution)/shard_map/ppermute | solution.py:411
  129.8 0.9 collective-permute-done.22
  131.1 2.2 %copy-done.5 = bf16[2,16,16,4096]{3,2,1,0:T(8,128)(2,1)S(1)} copy-done((bf16[2,16,16,4096]{3,2,1,0:T(8,128)(2,1)S(1)}, bf16[2,16,16,4096]{3,2,1,0:T(8,128)(2,1)}, u32[]{:S(2)}) %copy-start.5) | copy-done | bytes 4194328
  133.3 1.6 copy-done.9
  134.9 6.7 %mix_adjoint.1 = (f32[2,17,32,128]{3,2,1,0:T(8,128)S(1)}, f32[2,64,512]{2,1,0:T(8,128)S(1)}, f32[2,64,512]{2,1,0:T(8,128)S(1)}, f32[2,64,512]{2,1,0:T(8,128)S(1)}, f32[2,64,512]{2,1,0:T(8,128)S(1)}) custom-call(f32[2,32,512]{2,1,0:T(8,128)S(1)} %bitcast.37, f32[4,32,512]{2,1,0:T(8,128)S(1)} %bitcast.60, f32[2,32,512]{2,1,0:T(8,128)S(1)} %bitcast.38, ...), custom_call_target="tpu_custom_call" | custom-call | flops 9900000256 | bytes 31500000 | tf_op jit(solution)/shard_map/mix_adjoint/pallas_call | solution.py:466
  141.6 1.1 collective-permute-start.23
  142.7 1.5 collective-permute-start.27
  144.2 1.5 collective-permute-start.28
  146.1 2.0 %collective-permute-start.24 = (f32[2,8,8,512]{3,2,1,0:T(8,128)S(1)}, f32[2,8,8,512]{3,2,1,0:T(8,128)S(1)}, u32[]{:S(2)}, u32[]{:S(2)}) collective-permute-start(f32[2,8,8,512]{3,2,1,0:T(8,128)S(1)} %bitcast.54), channel_id=1, source_target_pairs={{0,4},{1,5},{2,6},{3,7},{4,0},{5,1},{6,2},{7,3},{8,12},{9,13},{10,... | collective-permute-start | bytes 786440 | tf_op jit(solution)/shard_map/ppermute | solution.py:411
  148.2 4.8 %collective-permute-done.23.refs_2_ = f32[2,8,8,512]{3,2,1,0:T(8,128)S(1)} collective-permute-done((f32[2,8,8,512]{3,2,1,0:T(8,128)S(1)}, f32[2,8,8,512]{3,2,1,0:T(8,128)S(1)}, u32[]{:S(2)}, u32[]{:S(2)}) %collective-permute-start.23) | collective-permute-done | bytes 262176 | tf_op jit(solution)/shard_map/ppermute | solution.py:411
  153.0 1.3 collective-permute-start.25
  154.3 13.2 %collective-permute-done.24.refs_4_ = f32[2,8,8,512]{3,2,1,0:T(8,128)S(1)} collective-permute-done((f32[2,8,8,512]{3,2,1,0:T(8,128)S(1)}, f32[2,8,8,512]{3,2,1,0:T(8,128)S(1)}, u32[]{:S(2)}, u32[]{:S(2)}) %collective-permute-start.24) | collective-permute-done | bytes 262176 | tf_op jit(solution)/shard_map/ppermute | solution.py:411
  168.4 1.9 collective-permute-done.28.refs_3_
  171.0 1.6 copy-done.6
  172.6 8.1 %weight_gradient.1 = f32[2,16,16,4096]{3,2,1,0:T(8,128)} custom-call(f32[4,2,16,32,128]{4,3,2,1,0:T(8,128)S(1)} %bitcast.48, f32[2,17,32,128]{3,2,1,0:T(8,128)S(1)} %get-tuple-element.100.refs_1_, f32[2,17,32,128]{3,2,1,0:T(8,128)S(1)} %collective-permute-done.27.refs_2_, f32[2,17,32,128]{3,2,1,0:T(8,128)S(1)} %collective-permute-done.28.refs_3_, ...), custom_call_target="tpu_custom_call" | custom-call | flops 9900000256 | bytes 31500000 | tf_op jit(solution)/shard_map/weight_gradient/pallas_call | solution.py:589
  180.7 7.3 %input_gradient.1 = bf16[1,8,16,128,128]{4,3,2,1,0:T(8,128)(2,1)} custom-call(f32[2,8,8,512]{3,2,1,0:T(8,128)S(1)} %bitcast.32, f32[4,8,8,512]{3,2,1,0:T(8,128)} %collective-permute-done.26.refs_1_.refs_3_.refs_5_.refs_7_, f32[2,8,8,512]{3,2,1,0:T(8,128)S(1)} %collective-permute-done.23.refs_2_, ...), custom_call_target="tpu_custom_call" | custom-call | flops 11000000512 | bytes 35000000 | tf_op jit(solution)/shard_map/input_gradient/pallas_call | solution.py:574
  (101 shorter events, 5.6 us)
Async XLA Ops:
  7.2 123.5 %all-gather.3.cloned.1.call-start = ((), (), s32[]{:S(2)}) async-start(), calls=%async_computation | async-start | bytes 2621440 | tf_op jit(solution)/shard_map/all_gather | solution.py:495
  7.2 2.2 %copy-start = (bf16[1,8,16,128,128]{4,3,2,1,0:T(8,128)(2,1)S(1)}, bf16[1,8,16,128,128]{4,3,2,1,0:T(8,128)(2,1)}, u32[]{:S(2)}) copy-start(bf16[1,8,16,128,128]{4,3,2,1,0:T(8,128)(2,1)} %refs_8_.5) | copy-start | bytes 12582916
  11.4 31.1 %copy-start.4 = (bf16[2,16,16,4096]{3,2,1,0:T(8,128)(2,1)S(1)}, bf16[2,16,16,4096]{3,2,1,0:T(8,128)(2,1)}, u32[]{:S(2)}) copy-start(bf16[2,16,16,4096]{3,2,1,0:T(8,128)(2,1)} %refs_17_.1) | copy-start | bytes 12582916
  11.4 31.1 %copy-start.8 = (bf16[2,512,1024]{2,1,0:T(8,128)(2,1)S(1)}, bf16[2,512,1024]{2,1,0:T(8,128)(2,1)}, u32[]{:S(2)}) copy-start(bf16[2,512,1024]{2,1,0:T(8,128)(2,1)} %constant.18.clone.refs_9_.refs_10_.refs_18_.refs_19_) | copy-start | bytes 6291460
  16.0 14.3 %collective-permute-start = (f32[2,8,8,512]{3,2,1,0:T(8,128)S(1)}, f32[2,8,8,512]{3,2,1,0:T(8,128)S(1)}, u32[]{:S(2)}, u32[]{:S(2)}) collective-permute-start(f32[2,8,8,512]{3,2,1,0:T(8,128)S(1)} %get-tuple-element.54), channel_id=1, source_target_pairs={{0,2},{1,3},{2,0},{3,1},{4,6},{5,7},{6,4},{7,5},{8,10},{9,11},{10,... | collective-permute-start | bytes 786440 | tf_op jit(solution)/shard_map/ppermute | solution.py:411
  19.1 21.4 %collective-permute-start.1 = (f32[2,8,8,512]{3,2,1,0:T(8,128)S(1)}, f32[2,8,8,512]{3,2,1,0:T(8,128)S(1)}, u32[]{:S(2)}, u32[]{:S(2)}) collective-permute-start(f32[2,8,8,512]{3,2,1,0:T(8,128)S(1)} %get-tuple-element.55), channel_id=1, source_target_pairs={{0,4},{1,5},{2,6},{3,7},{4,0},{5,1},{6,2},{7,3},{8,12},{9,13},{10,... | collective-permute-start | bytes 786440 | tf_op jit(solution)/shard_map/ppermute | solution.py:411
  21.7 18.8 %collective-permute-start.2 = (f32[2,8,8,512]{3,2,1,0:T(8,128)S(1)}, f32[2,8,8,512]{3,2,1,0:T(8,128)S(1)}, u32[]{:S(2)}, u32[]{:S(2)}) collective-permute-start(f32[2,8,8,512]{3,2,1,0:T(8,128)S(1)} %get-tuple-element.56), channel_id=1, source_target_pairs={{0,6},{1,7},{2,4},{3,5},{4,2},{5,3},{6,0},{7,1},{8,14},{9,15},{10,... | collective-permute-start | bytes 786440 | tf_op jit(solution)/shard_map/ppermute | solution.py:411
  40.5 2.0 %collective-permute-start.3 = (f32[4,8,8,512]{3,2,1,0:T(8,128)S(1)}, f32[4,8,8,512]{3,2,1,0:T(8,128)S(1)}, u32[]{:S(2)}, u32[]{:S(2)}) collective-permute-start(f32[4,8,8,512]{3,2,1,0:T(8,128)S(1)} %pad_maximum_fusion), channel_id=1, source_target_pairs={{0,1},{1,0},{2,3},{3,2},{4,5},{5,4},{6,7},{7,6},{8,9},{9,8},{10,11... | collective-permute-start | bytes 1572872 | tf_op jit(solution)/shard_map/ppermute | solution.py:411
  42.5 29.6 %copy-start.7 = (bf16[16,16]{1,0:T(8,128)(2,1)S(1)}, bf16[16,16]{1,0:T(8,128)(2,1)}, u32[]{:S(2)}) copy-start(bf16[16,16]{1,0:T(8,128)(2,1)} %refs_10_.5) | copy-start | bytes 1540
  42.5 29.6 %copy-start.10 = (bf16[768,512]{1,0:T(8,128)(2,1)S(1)}, bf16[768,512]{1,0:T(8,128)(2,1)}, u32[]{:S(2)}) copy-start(bf16[768,512]{1,0:T(8,128)(2,1)} %constant.15.clone.refs_14_.refs_9_) | copy-start | bytes 2359300
  42.5 29.6 %copy-start.13 = (bf16[1536,256]{1,0:T(8,128)(2,1)S(1)}, bf16[1536,256]{1,0:T(8,128)(2,1)}, u32[]{:S(2)}) copy-start(bf16[1536,256]{1,0:T(8,128)(2,1)} %constant.14.clone.y_fwd_ref.refs_12_) | copy-start | bytes 2359300
  42.5 29.6 %copy-start.14 = (bf16[256,256]{1,0:T(8,128)(2,1)S(1)}, bf16[256,256]{1,0:T(8,128)(2,1)}, u32[]{:S(2)}) copy-start(bf16[256,256]{1,0:T(8,128)(2,1)} %constant.17.clone.refs_15_.refs_10_) | copy-start | bytes 393220
  49.3 10.5 %collective-permute-start.4 = (f32[2,4,8,512]{3,2,1,0:T(8,128)S(1)}, f32[2,4,8,512]{3,2,1,0:T(8,128)S(1)}, u32[]{:S(2)}, u32[]{:S(2)}) collective-permute-start(f32[2,4,8,512]{3,2,1,0:T(8,128)S(1)} %bitcast.69), channel_id=1, source_target_pairs={{0,2},{1,3},{2,0},{3,1},{4,6},{5,7},{6,4},{7,5},{8,10},{9,11},{10,... | collective-permute-start | bytes 393224 | tf_op jit(solution)/shard_map/ppermute | solution.py:411
  54.0 12.9 %collective-permute-start.5 = (f32[2,4,8,512]{3,2,1,0:T(8,128)S(1)}, f32[2,4,8,512]{3,2,1,0:T(8,128)S(1)}, u32[]{:S(2)}, u32[]{:S(2)}) collective-permute-start(f32[2,4,8,512]{3,2,1,0:T(8,128)S(1)} %bitcast.68), channel_id=1, source_target_pairs={{0,4},{1,5},{2,6},{3,7},{4,0},{5,1},{6,2},{7,3},{8,12},{9,13},{10,... | collective-permute-start | bytes 393224 | tf_op jit(solution)/shard_map/ppermute | solution.py:411
  55.2 11.8 %collective-permute-start.6 = (f32[2,4,8,512]{3,2,1,0:T(8,128)S(1)}, f32[2,4,8,512]{3,2,1,0:T(8,128)S(1)}, u32[]{:S(2)}, u32[]{:S(2)}) collective-permute-start(f32[2,4,8,512]{3,2,1,0:T(8,128)S(1)} %bitcast.67), channel_id=1, source_target_pairs={{0,6},{1,7},{2,4},{3,5},{4,2},{5,3},{6,0},{7,1},{8,14},{9,15},{10,... | collective-permute-start | bytes 393224 | tf_op jit(solution)/shard_map/ppermute | solution.py:411
  67.7 4.4 %collective-permute-start.7 = (f32[4,4,8,512]{3,2,1,0:T(8,128)}, f32[4,4,8,512]{3,2,1,0:T(8,128)S(1)}, u32[]{:S(2)}, u32[]{:S(2)}) collective-permute-start(f32[4,4,8,512]{3,2,1,0:T(8,128)} %pad_maximum_fusion.2), channel_id=1, source_target_pairs={{0,1},{1,0},{2,3},{3,2},{4,5},{5,4},{6,7},{7,6},{8,9},{9,8},{10,11... | collective-permute-start | bytes 786440 | tf_op jit(solution)/shard_map/ppermute | solution.py:411
  67.7 24.6 %collective-permute-start.10 = (f32[2,4,8,512]{3,2,1,0:T(8,128)S(1)}, f32[2,4,8,512]{3,2,1,0:T(8,128)S(1)}, u32[]{:S(2)}, u32[]{:S(2)}) collective-permute-start(f32[2,4,8,512]{3,2,1,0:T(8,128)S(1)} %bitcast.66), channel_id=1, source_target_pairs={{0,6},{1,7},{2,4},{3,5},{4,2},{5,3},{6,0},{7,1},{8,14},{9,15},{10,... | collective-permute-start | bytes 393224 | tf_op jit(solution)/shard_map/ppermute | solution.py:411
  70.0 22.3 %collective-permute-start.8 = (f32[2,4,8,512]{3,2,1,0:T(8,128)S(1)}, f32[2,4,8,512]{3,2,1,0:T(8,128)S(1)}, u32[]{:S(2)}, u32[]{:S(2)}) collective-permute-start(f32[2,4,8,512]{3,2,1,0:T(8,128)S(1)} %bitcast.65), channel_id=1, source_target_pairs={{0,2},{1,3},{2,0},{3,1},{4,6},{5,7},{6,4},{7,5},{8,10},{9,11},{10,... | collective-permute-start | bytes 393224 | tf_op jit(solution)/shard_map/ppermute | solution.py:411
  71.5 20.7 %collective-permute-start.9 = (f32[2,4,8,512]{3,2,1,0:T(8,128)S(1)}, f32[2,4,8,512]{3,2,1,0:T(8,128)S(1)}, u32[]{:S(2)}, u32[]{:S(2)}) collective-permute-start(f32[2,4,8,512]{3,2,1,0:T(8,128)S(1)} %bitcast.64), channel_id=1, source_target_pairs={{0,4},{1,5},{2,6},{3,7},{4,0},{5,1},{6,2},{7,3},{8,12},{9,13},{10,... | collective-permute-start | bytes 393224 | tf_op jit(solution)/shard_map/ppermute | solution.py:411
  72.2 2.2 %copy-start.1 = (bf16[1,8,16,128,128]{4,3,2,1,0:T(8,128)(2,1)S(1)}, bf16[1,8,16,128,128]{4,3,2,1,0:T(8,128)(2,1)}, u32[]{:S(2)}) copy-start(bf16[1,8,16,128,128]{4,3,2,1,0:T(8,128)(2,1)} %refs_8_.5) | copy-start | bytes 12582916
  74.4 2.2 %copy-start.2 = (bf16[1,8,16,128,128]{4,3,2,1,0:T(8,128)(2,1)S(1)}, bf16[1,8,16,128,128]{4,3,2,1,0:T(8,128)(2,1)}, u32[]{:S(2)}) copy-start(bf16[1,8,16,128,128]{4,3,2,1,0:T(8,128)(2,1)} %refs_9_.5) | copy-start | bytes 12582916
  78.2 18.7 %copy-start.3 = (bf16[1,8,16,128,128]{4,3,2,1,0:T(8,128)(2,1)S(1)}, bf16[1,8,16,128,128]{4,3,2,1,0:T(8,128)(2,1)}, u32[]{:S(2)}) copy-start(bf16[1,8,16,128,128]{4,3,2,1,0:T(8,128)(2,1)} %refs_9_.5) | copy-start | bytes 12582916
  92.4 4.5 %collective-permute-start.11 = (f32[4,4,8,512]{3,2,1,0:T(8,128)S(1)}, f32[4,4,8,512]{3,2,1,0:T(8,128)S(1)}, u32[]{:S(2)}, u32[]{:S(2)}) collective-permute-start(f32[4,4,8,512]{3,2,1,0:T(8,128)S(1)} %pad_maximum_fusion.3), channel_id=1, source_target_pairs={{0,1},{1,0},{2,3},{3,2},{4,5},{5,4},{6,7},{7,6},{8,9},{9,8},{10,11... | collective-permute-start | bytes 786440 | tf_op jit(solution)/shard_map/ppermute | solution.py:411
  92.4 21.9 %collective-permute-start.12 = (f32[2,4,8,512]{3,2,1,0:T(8,128)S(1)}, f32[2,4,8,512]{3,2,1,0:T(8,128)S(1)}, u32[]{:S(2)}, u32[]{:S(2)}) collective-permute-start(f32[2,4,8,512]{3,2,1,0:T(8,128)S(1)} %get-tuple-element.78), channel_id=1, source_target_pairs={{0,2},{1,3},{2,0},{3,1},{4,6},{5,7},{6,4},{7,5},{8,10},{9,11},{10,... | collective-permute-start | bytes 393224 | tf_op jit(solution)/shard_map/ppermute | solution.py:411
  93.9 20.4 %collective-permute-start.13 = (f32[2,4,8,512]{3,2,1,0:T(8,128)S(1)}, f32[2,4,8,512]{3,2,1,0:T(8,128)S(1)}, u32[]{:S(2)}, u32[]{:S(2)}) collective-permute-start(f32[2,4,8,512]{3,2,1,0:T(8,128)S(1)} %get-tuple-element.79), channel_id=1, source_target_pairs={{0,4},{1,5},{2,6},{3,7},{4,0},{5,1},{6,2},{7,3},{8,12},{9,13},{10,... | collective-permute-start | bytes 393224 | tf_op jit(solution)/shard_map/ppermute | solution.py:411
  95.4 18.9 %collective-permute-start.14 = (f32[2,4,8,512]{3,2,1,0:T(8,128)S(1)}, f32[2,4,8,512]{3,2,1,0:T(8,128)S(1)}, u32[]{:S(2)}, u32[]{:S(2)}) collective-permute-start(f32[2,4,8,512]{3,2,1,0:T(8,128)S(1)} %get-tuple-element.80), channel_id=1, source_target_pairs={{0,6},{1,7},{2,4},{3,5},{4,2},{5,3},{6,0},{7,1},{8,14},{9,15},{10,... | collective-permute-start | bytes 393224 | tf_op jit(solution)/shard_map/ppermute | solution.py:411
  111.0 3.3 %copy-start.19 = (f32[8,16,128,128]{3,2,1,0:T(8,128)}, f32[8,16,128,128]{3,2,1,0:T(8,128)S(1)}, u32[]{:S(2)}) copy-start(f32[8,16,128,128]{3,2,1,0:T(8,128)S(1)} %get-tuple-element.99.refs_8_) | copy-start | bytes 25165828
  114.3 14.7 %collective-permute-start.19 = (f32[2,4,8,512]{3,2,1,0:T(8,128)S(1)}, f32[2,4,8,512]{3,2,1,0:T(8,128)S(1)}, u32[]{:S(2)}, u32[]{:S(2)}) collective-permute-start(f32[2,4,8,512]{3,2,1,0:T(8,128)S(1)} %get-tuple-element.89), channel_id=1, source_target_pairs={{0,2},{1,3},{2,0},{3,1},{4,6},{5,7},{6,4},{7,5},{8,10},{9,11},{10,... | collective-permute-start | bytes 393224 | tf_op jit(solution)/shard_map/ppermute | solution.py:411
  114.9 14.1 %collective-permute-start.20 = (f32[2,4,8,512]{3,2,1,0:T(8,128)S(1)}, f32[2,4,8,512]{3,2,1,0:T(8,128)S(1)}, u32[]{:S(2)}, u32[]{:S(2)}) collective-permute-start(f32[2,4,8,512]{3,2,1,0:T(8,128)S(1)} %get-tuple-element.90), channel_id=1, source_target_pairs={{0,4},{1,5},{2,6},{3,7},{4,0},{5,1},{6,2},{7,3},{8,12},{9,13},{10,... | collective-permute-start | bytes 393224 | tf_op jit(solution)/shard_map/ppermute | solution.py:411
  117.3 11.8 %collective-permute-start.21 = (f32[2,4,8,512]{3,2,1,0:T(8,128)S(1)}, f32[2,4,8,512]{3,2,1,0:T(8,128)S(1)}, u32[]{:S(2)}, u32[]{:S(2)}) collective-permute-start(f32[2,4,8,512]{3,2,1,0:T(8,128)S(1)} %get-tuple-element.91), channel_id=1, source_target_pairs={{0,6},{1,7},{2,4},{3,5},{4,2},{5,3},{6,0},{7,1},{8,14},{9,15},{10,... | collective-permute-start | bytes 393224 | tf_op jit(solution)/shard_map/ppermute | solution.py:411
  118.8 1.1 collective-permute-start.16
  120.0 3.6 %collective-permute-start.17 = (f32[2,128]{1,0:T(2,128)S(1)}, f32[2,128]{1,0:T(2,128)S(1)}, u32[]{:S(2)}, u32[]{:S(2)}) collective-permute-start(f32[2,128]{1,0:T(2,128)S(1)} %add.28), channel_id=1, source_target_pairs={{0,2},{1,3},{2,0},{3,1},{4,6},{5,7},{6,4},{7,5},{8,10},{9,11},{10,... | collective-permute-start | bytes 3080 | tf_op jit(solution)/shard_map/ppermute | solution.py:411
  123.6 5.4 %collective-permute-start.18 = (f32[2,128]{1,0:T(2,128)S(1)}, f32[2,128]{1,0:T(2,128)S(1)}, u32[]{:S(2)}, u32[]{:S(2)}) collective-permute-start(f32[2,128]{1,0:T(2,128)S(1)} %add.29), channel_id=1, source_target_pairs={{0,4},{1,5},{2,6},{3,7},{4,0},{5,1},{6,2},{7,3},{8,12},{9,13},{10,... | collective-permute-start | bytes 3080 | tf_op jit(solution)/shard_map/ppermute | solution.py:411
  129.1 1.6 collective-permute-start.22
  129.2 1.9 collective-permute-start.15
  131.1 2.2 %copy-start.5 = (bf16[2,16,16,4096]{3,2,1,0:T(8,128)(2,1)S(1)}, bf16[2,16,16,4096]{3,2,1,0:T(8,128)(2,1)}, u32[]{:S(2)}) copy-start(bf16[2,16,16,4096]{3,2,1,0:T(8,128)(2,1)} %refs_17_.1) | copy-start | bytes 12582916
  133.3 1.6 copy-start.9
  141.6 11.4 %collective-permute-start.23 = (f32[2,8,8,512]{3,2,1,0:T(8,128)S(1)}, f32[2,8,8,512]{3,2,1,0:T(8,128)S(1)}, u32[]{:S(2)}, u32[]{:S(2)}) collective-permute-start(f32[2,8,8,512]{3,2,1,0:T(8,128)S(1)} %bitcast.59), channel_id=1, source_target_pairs={{0,2},{1,3},{2,0},{3,1},{4,6},{5,7},{6,4},{7,5},{8,10},{9,11},{10,... | collective-permute-start | bytes 786440 | tf_op jit(solution)/shard_map/ppermute | solution.py:411
  142.7 25.7 %collective-permute-start.27 = (f32[2,17,32,128]{3,2,1,0:T(8,128)S(1)}, f32[2,17,32,128]{3,2,1,0:T(8,128)S(1)}, u32[]{:S(2)}, u32[]{:S(2)}) collective-permute-start(f32[2,17,32,128]{3,2,1,0:T(8,128)S(1)} %get-tuple-element.100.refs_1_), channel_id=1, source_target_pairs={{0,8},{8,0},{16,24},{24,16},{1,9},{9,1},{17,25},{25,17},{2,10},{10... | collective-permute-start | bytes 1671176 | tf_op jit(solution)/shard_map/ppermute | solution.py:442
  144.2 26.1 %collective-permute-start.28 = (f32[2,17,32,128]{3,2,1,0:T(8,128)S(1)}, f32[2,17,32,128]{3,2,1,0:T(8,128)S(1)}, u32[]{:S(2)}, u32[]{:S(2)}) collective-permute-start(f32[2,17,32,128]{3,2,1,0:T(8,128)S(1)} %get-tuple-element.100.refs_1_), channel_id=1, source_target_pairs={{0,16},{8,24},{16,0},{24,8},{1,17},{9,25},{17,1},{25,9},{2,18},{10... | collective-permute-start | bytes 1671176 | tf_op jit(solution)/shard_map/ppermute | solution.py:442
  145.7 24.6 %collective-permute-start.29 = (f32[2,17,32,128]{3,2,1,0:T(8,128)S(1)}, f32[2,17,32,128]{3,2,1,0:T(8,128)S(1)}, u32[]{:S(2)}, u32[]{:S(2)}) collective-permute-start(f32[2,17,32,128]{3,2,1,0:T(8,128)S(1)} %get-tuple-element.100.refs_1_), channel_id=1, source_target_pairs={{0,24},{8,16},{16,8},{24,0},{1,25},{9,17},{17,9},{25,1},{2,26},{10... | collective-permute-start | bytes 1671176 | tf_op jit(solution)/shard_map/ppermute | solution.py:442
  146.1 21.4 %collective-permute-start.24 = (f32[2,8,8,512]{3,2,1,0:T(8,128)S(1)}, f32[2,8,8,512]{3,2,1,0:T(8,128)S(1)}, u32[]{:S(2)}, u32[]{:S(2)}) collective-permute-start(f32[2,8,8,512]{3,2,1,0:T(8,128)S(1)} %bitcast.54), channel_id=1, source_target_pairs={{0,4},{1,5},{2,6},{3,7},{4,0},{5,1},{6,2},{7,3},{8,12},{9,13},{10,... | collective-permute-start | bytes 786440 | tf_op jit(solution)/shard_map/ppermute | solution.py:411
  153.0 14.5 %collective-permute-start.25 = (f32[2,8,8,512]{3,2,1,0:T(8,128)S(1)}, f32[2,8,8,512]{3,2,1,0:T(8,128)S(1)}, u32[]{:S(2)}, u32[]{:S(2)}) collective-permute-start(f32[2,8,8,512]{3,2,1,0:T(8,128)S(1)} %bitcast.53), channel_id=1, source_target_pairs={{0,6},{1,7},{2,4},{3,5},{4,2},{5,3},{6,0},{7,1},{8,14},{9,15},{10,... | collective-permute-start | bytes 786440 | tf_op jit(solution)/shard_map/ppermute | solution.py:411
  168.4 12.3 %collective-permute-start.26 = (f32[4,8,8,512]{3,2,1,0:T(8,128)}, f32[4,8,8,512]{3,2,1,0:T(8,128)}, u32[]{:S(2)}, u32[]{:S(2)}) collective-permute-start(f32[4,8,8,512]{3,2,1,0:T(8,128)} %pad_maximum_fusion.1), channel_id=1, source_target_pairs={{0,1},{1,0},{2,3},{3,2},{4,5},{5,4},{6,7},{7,6},{8,9},{9,8},{10,11... | collective-permute-start | bytes 1572872 | tf_op jit(solution)/shard_map/ppermute | solution.py:411
  171.0 1.6 copy-start.6
  172.6 8.1 %copy-start.11 = (bf16[768,512]{1,0:T(8,128)(2,1)S(1)}, bf16[768,512]{1,0:T(8,128)(2,1)}, u32[]{:S(2)}) copy-start(bf16[768,512]{1,0:T(8,128)(2,1)} %constant.15.clone.refs_14_.refs_9_) | copy-start | bytes 2359300
  172.6 8.1 %copy-start.15 = (bf16[256,256]{1,0:T(8,128)(2,1)S(1)}, bf16[256,256]{1,0:T(8,128)(2,1)}, u32[]{:S(2)}) copy-start(bf16[256,256]{1,0:T(8,128)(2,1)} %constant.17.clone.refs_15_.refs_10_) | copy-start | bytes 393220
  172.6 8.1 %copy-start.20 = (f32[8,16,128,128]{3,2,1,0:T(8,128)S(1)}, f32[8,16,128,128]{3,2,1,0:T(8,128)}, u32[]{:S(2)}) copy-start(f32[8,16,128,128]{3,2,1,0:T(8,128)} %copy-done.19) | copy-start | bytes 25165828
  (4 other events, 3.7 us)
Sparse Core Ops, SparseCore 0:
  72.2 35.3 all-gather.2
